TPU v7x, 128 devices: a whole 4x4x4 slice. The times are simulated.
128 devices in a mesh: tm: 32 (over x, z, core), state: 4 (over y).
Axes of the slice: x: 4, y: 4, z: 4, core: 2. Of those that a mesh axis runs over, the one named last changes fastest.
Arguments:
- dyn_cols: int32 [1024, 8, 3], P('tm', 'state'), may hold values from 0 to 7, as said below
- dyn_vals: bfloat16 [1024, 8, 64, 192], P('tm', 'state'), may hold values from -1 to 1
- obs_blocks: int32 [1024, 2], P('tm'), may hold values from 0 to 7
- obs_op: bfloat16 [1024, 64, 128], P('tm'), may hold values from -0.75 to 0.75
- obs_counts: int32 [1024], P('tm'), may hold values from 32 to 128, as said below
- obs_values: float32 [1024, 128], P('tm'), may hold values from -6 to 6
- gain: bfloat16 [1024, 512, 128], P('tm', 'state'), may hold values from -0.0078125 to 0.0078125
- sources: float32 [1024, 512], P('tm', 'state'), may hold values from -0.625 to 0.625
- prior: float32 [512], replicated, may hold values from -6 to 6
Outputs:
- filtered: float32 [1024, 512], P('tm', 'state')
Inputs may be any that keep to these rules, and one draw needn't show every extreme that they name: `dyn_cols`: for every step and block row i, the first entry is i itself and the 3 entries are distinct block columns. `obs_counts`: some step has all 128 observations present.
All inputs are finite; a program needn't handle non-finite values.
Results may differ from a plain program's by a relative error of at most 0.0003.
The roundings to bfloat16 on the way count: a program that leaves them out, or rounds other values in their place, can miss the bound.
Values may be sent and summed in bfloat16 or wider, within the bound.
A program may use at most 128 MiB of HBM per device.

v0:
```python
import jax
import jax.numpy as jnp
from jax import lax
from jax.sharding import PartitionSpec as P

NS = 512
BS = 64
KF = 3
OBS = 128
NB = 8
OB = 2


HIGHEST = lax.Precision.HIGHEST


def prefix(value, axis, join, neutral):
    count, mine = (lax.axis_size(axis), lax.axis_index(axis))
    pieces = jax.tree.map(lambda part: lax.all_gather(part, axis), value)
    so_far = jax.tree.map(
        lambda part, zero: jnp.full_like(part, 0) + jnp.asarray(zero, part.dtype), value, neutral
    )

    def step(position, so_far):
        longer = join(so_far, jax.tree.map(lambda part: part[position], pieces))
        return jax.tree.map(lambda new, old: jnp.where(position < mine, new, old), longer, so_far)

    return lax.fori_loop(0, count - 1, step, so_far)


def split_product(matrix, operand):
    leading = operand.astype(jnp.bfloat16)
    remainder = (operand - lax.optimization_barrier(leading).astype(jnp.float32)).astype(
        jnp.bfloat16
    )
    return jnp.dot(matrix, leading, preferred_element_type=jnp.float32) + jnp.dot(
        matrix, remainder, preferred_element_type=jnp.float32
    )


def body(dyn_cols, dyn_vals, obs_blocks, obs_op, obs_counts, obs_values, gain, sources, prior):
    step_count = dyn_vals.shape[0]
    local_blocks = dyn_vals.shape[1]
    local_rows = local_blocks * BS
    state_index = lax.axis_index("state")
    onehot = (dyn_cols[..., None] == jnp.arange(NB)).astype(jnp.bfloat16)
    blocks = dyn_vals.reshape(step_count, local_blocks, BS, KF, BS)
    forward = jnp.einsum("tikc,tiakb->tiacb", onehot, blocks, preferred_element_type=jnp.float32)
    forward = forward.reshape(step_count, local_blocks, BS, NS)
    forward_narrow = forward.astype(jnp.bfloat16)
    owned = state_index * local_blocks + jnp.arange(local_blocks)
    select = obs_blocks[:, :, None] == owned[None, None, :]
    selected = jnp.einsum(
        "tos,tsbn->tobn",
        select.astype(jnp.bfloat16),
        forward_narrow,
        preferred_element_type=jnp.float32,
    ).astype(jnp.bfloat16)
    operator_blocks = obs_op.reshape(step_count, BS, OB, BS)
    image_part = jnp.einsum(
        "tboa,tobn->toan", operator_blocks, selected, preferred_element_type=jnp.float32
    )
    image_part = image_part.reshape(step_count, OBS, NS)
    source_sel = jnp.einsum(
        "tos,tsb->tob",
        select.astype(jnp.float32),
        sources.reshape(step_count, local_blocks, BS),
        precision=HIGHEST,
    )
    source_part = jnp.einsum(
        "tboa,tob->toa", operator_blocks.astype(jnp.float32), source_sel, precision=HIGHEST
    )
    source_part = source_part.reshape(step_count, OBS)
    image_sum, source_sum = (
        lax.psum(image_part.astype(jnp.bfloat16), "state").astype(jnp.float32),
        lax.psum(source_part.astype(jnp.bfloat16), "state").astype(jnp.float32),
    )
    active = jnp.arange(OBS)[None, :] < obs_counts[:, None]
    masked = jnp.where(
        active[:, :, None], image_sum.astype(jnp.bfloat16), jnp.zeros((), jnp.bfloat16)
    )
    source_image = lax.optimization_barrier(source_sum.astype(jnp.bfloat16)).astype(jnp.float32)
    innovation = jnp.where(active, obs_values - source_image, 0.0)
    correction = jnp.einsum("tro,ton->trn", gain, masked, preferred_element_type=jnp.float32)
    element = (forward.reshape(step_count, local_rows, NS) - correction).astype(jnp.bfloat16)
    offset = sources + jnp.einsum(
        "tro,to->tr", gain.astype(jnp.float32), innovation, precision=HIGHEST
    )
    full_elements = lax.all_gather(element, "state", axis=1, tiled=True)
    full_offsets = lax.all_gather(offset, "state", axis=1, tiled=True)
    start_cols = (
        jnp.arange(NS)[:, None] == (state_index * local_rows + jnp.arange(local_rows))[None, :]
    ).astype(jnp.float32)

    def compose(carry, inputs):
        product, vector = carry
        matrix, shift_term = inputs
        product = split_product(matrix, product)
        vector = split_product(matrix, vector) + shift_term
        return ((product, vector), None)

    (column_product, span_offset), _ = lax.scan(
        compose, (start_cols, jnp.zeros((NS,), jnp.float32)), (full_elements, full_offsets)
    )
    span_matrix = lax.all_gather(column_product, "state", axis=1, tiled=True)

    def combine(earlier, later):
        return (
            jnp.dot(later[0], earlier[0], precision=HIGHEST),
            jnp.dot(later[0], earlier[1], precision=HIGHEST) + later[1],
        )

    identity = (jnp.eye(NS, dtype=jnp.float32), jnp.zeros((NS,), jnp.float32))
    before = prefix((span_matrix, span_offset), "tm", combine, identity)
    entry = jnp.dot(before[0], prior, precision=HIGHEST) + before[1]

    def sweep(current, inputs):
        matrix, shift_term = inputs
        new_mean = split_product(matrix, current) + shift_term
        return (new_mean, lax.dynamic_slice_in_dim(new_mean, state_index * local_rows, local_rows))

    _, filtered = lax.scan(sweep, entry, (full_elements, full_offsets))
    return filtered


def solution(mesh):
    return jax.shard_map(
        body,
        mesh=mesh,
        in_specs=(
            P("tm", "state", None),
            P("tm", "state", None, None),
            P("tm", None),
            P("tm", None, None),
            P("tm"),
            P("tm", None),
            P("tm", "state", None),
            P("tm", "state"),
            P(),
        ),
        out_specs=P("tm", "state"),
        check_vma=False,
    )
```

profile of v0, /device:TPU:103, one launch (start us, length us, event | category | flops | bytes accessed | tf_op | source)
XLA Modules:
  0.0 962.8 jit_solution(8072769552737119339)
XLA Ops:
  6.5 4.6 copy.27
  11.1 7.2 copy.28
  18.4 10.6 %fusion.58 = (bf16[32,2,64,8,64]{4,3,2,1,0:T(8,128)(2,1)}, f32[32,2,64,8,64]{4,3,2,1,0:T(8,128)}) fusion(bf16[32,2,64,3,64]{4,3,2,1,0:T(4,128)(2,1)} %copy.28, s32[32,2,3]{2,1,0:T(2,128)S(1)} %copy.26), kind=kOutput, calls=%fused_computation.79 | convolution fusion | flops 14681600 | bytes 14156544 | tf_op jit(solution)/shard_map/tikc,tiakb->tiacb/dot_general | solution.py:48
  29.0 11.9 %convert_element_type.81 = bf16[32,2,64,512]{3,2,1,0:T(8,128)(2,1)} reshape(bf16[32,2,64,8,64]{4,3,2,1,0:T(8,128)(2,1)} %get-tuple-element.329) | data formatting | bytes 8388608 | tf_op jit(solution)/shard_map/convert_element_type | solution.py:50
  41.4 8.7 convolution_convert_fusion
  50.2 3.2 fusion.39
  53.4 6.4 copy.33
  59.9 14.6 %reshape_reshape.3 = f32[32,128,512]{2,1,0:T(8,128)} reshape(f32[32,2,64,8,64]{4,3,2,1,0:T(8,128)} %get-tuple-element.330) | data formatting | bytes 16777216 | tf_op jit(solution)/shard_map/reshape;reshape | solution.py:85
  74.5 9.0 copy.34
  83.6 70.4 %all-reduce.2.cloned.1.call-done = bf16[32,128,512]{1,2,0:T(8,128)(2,1)} async-done(((bf16[32,128,512]{1,2,0:T(8,128)(2,1)}), bf16[32,128,512]{1,2,0:T(8,128)(2,1)}) %all-reduce.2.cloned.1.call-update) | async-done | bytes 4194320 | tf_op jit(solution)/shard_map/psum | solution.py:75
  154.1 7.9 fusion.30
  163.5 6.6 psum.15
  171.9 9.6 all_gather.22
  181.5 138.3 %all-gather.7.cloned.1.call-done = bf16[32,512,512]{1,2,0:T(8,128)(2,1)} async-done(((bf16[32,128,512]{1,2,0:T(8,128)(2,1)}), bf16[32,512,512]{1,2,0:T(8,128)(2,1)}) %all-gather.7.cloned.1.call-update) | async-done | bytes 16777232 | tf_op jit(solution)/shard_map/all_gather | solution.py:89
  319.8 22.6 %copy.35 = bf16[32,512,512]{2,1,0:T(8,128)(2,1)} copy(bf16[32,512,512]{1,2,0:T(8,128)(2,1)} %all-gather.7.cloned.1.call-done) | data formatting | bytes 33554432
  342.4 173.2 %while.47 = (s32[]{:T(128)}, f32[512,128]{1,0:T(8,128)S(1)}, f32[512]{0:T(512)S(1)}, bf16[32,512,512]{2,1,0:T(8,128)(2,1)}, f32[32,512]{1,0:T(8,128)S(1)}) while((s32[]{:T(128)}, f32[512,128]{1,0:T(8,128)S(1)}, f32[512]{0:T(512)S(1)}, bf16[32,512,512]{2,1,0:T(8,128)(2,1)}, f32[32,512]{1,0:T(8,128)S(1)}) %tuple.85), condition=%wide.region_3.4_spmd.clone.clone, body=%wide.region_2.3_spmd.clone.sunk.clone | while | flops 135597568 | bytes 4357196 | solution.py:102
  516.5 26.3 %all-gather.9.cloned.1.call-done = f32[512,512]{1,0:T(8,128)} async-done(((f32[512,128]{1,0:T(8,128)}), f32[512,512]{1,0:T(8,128)}) %all-gather.9.cloned.1.call-update) | async-done | bytes 1048592 | tf_op jit(solution)/shard_map/all_gather | solution.py:105
  542.9 23.3 %all-gather.2 = f32[32,1,512]{2,1,0:T(1,128)S(1)} all-gather(f32[1,1,512]{2,1,0:T(1,128)S(1)} %bitcast.166), channel_id=3, replica_groups=mesh['tm'=32,'state'=4] {'tm'}, dimensions={0}, use_global_device_ids=true | all-gather | bytes 67584 | tf_op jit(solution)/shard_map/all_gather | solution.py:19
  566.2 92.9 %all-gather.11.cloned.1.call-done = f32[16384,512]{1,0:T(8,128)} async-done(((f32[512,512]{1,0:T(8,128)}), f32[16384,512]{1,0:T(8,128)}) %all-gather.11.cloned.1.call-update) | async-done | bytes 33554448 | tf_op jit(solution)/shard_map/all_gather | solution.py:19
  659.2 168.3 %while.48 = (s32[]{:T(128)}, f32[512,512]{1,0:T(8,128)S(1)}, f32[512]{0:T(512)S(1)}, s32[]{:T(128)}, f32[32,512,512]{2,1,0:T(8,128)}, /*index=5*/f32[32,512]{1,0:T(8,128)S(1)}) while((s32[]{:T(128)}, f32[512,512]{1,0:T(8,128)S(1)}, f32[512]{0:T(512)S(1)}, s32[]{:T(128)}, f32[32,512,512]{2,1,0:T(8,128)}, ...), condition=%wide.region_5.6_spmd.clone.clone, body=%wide.region_4.5_spmd.clone.sunk.clone | while | flops 1614022656 | bytes 7361631 | solution.py:28
  666.9 3.1 convolution_select_fusion.3
  672.4 3.1 convolution_select_fusion.3
  699.5 3.1 convolution_select_fusion.3
  828.5 127.8 %while.46 = (s32[]{:T(128)}, f32[512]{0:T(512)S(1)}, f32[32,128]{1,0:T(8,128)}, bf16[32,512,512]{2,1,0:T(8,128)(2,1)}, f32[32,512]{1,0:T(8,128)S(1)}, /*index=5*/s32[]{:T(128)}) while((s32[]{:T(128)}, f32[512]{0:T(512)S(1)}, f32[32,128]{1,0:T(8,128)}, bf16[32,512,512]{2,1,0:T(8,128)(2,1)}, f32[32,512]{1,0:T(8,128)S(1)}, ...), condition=%wide.region_7.8_spmd.clone, body=%wide.region_6.7_spmd.sunk.clone | while | flops 1051650 | bytes 1081425 | solution.py:122
  (935 shorter events, 461.8 us)
Async XLA Ops:
  6.5 147.5 %copy-start = (bf16[32,128,128]{2,1,0:T(8,128)(2,1)S(1)}, bf16[32,128,128]{2,1,0:T(8,128)(2,1)}, u32[]{:S(2)}) copy-start(bf16[32,128,128]{2,1,0:T(8,128)(2,1)} %param.21) | copy-start | bytes 3145732
  6.5 11.7 %copy-start.5 = (s32[32,2,3]{0,1,2:T(2,128)S(1)}, s32[32,2,3]{0,1,2:T(2,128)}, u32[]{:S(2)}) copy-start(s32[32,2,3]{0,1,2:T(2,128)} %param.15) | copy-start | bytes 2308
  6.5 147.5 %all-reduce.2.cloned.1.call-start = ((), (), s32[]{:S(2)}) async-start(), calls=%async_computation | async-start | bytes 8388608 | tf_op jit(solution)/shard_map/psum | solution.py:75
  29.0 11.9 %copy-start.8 = (s32[32,2]{0,1:T(2,128)S(1)}, s32[32,2]{0,1:T(2,128)}, u32[]{:S(2)}) copy-start(s32[32,2]{0,1:T(2,128)} %param.17) | copy-start | bytes 772
  29.0 12.0 %copy-start.2 = (bf16[32,64,128]{2,1,0:T(8,128)(2,1)S(1)}, bf16[32,64,128]{2,1,0:T(8,128)(2,1)}, u32[]{:S(2)}) copy-start(bf16[32,64,128]{2,1,0:T(8,128)(2,1)} %param.18) | copy-start | bytes 1572868
  59.9 259.9 %all-gather.7.cloned.1.call-start = ((), (), s32[]{:S(2)}) async-start(), calls=%async_computation.1 | async-start | bytes 20971520 | tf_op jit(solution)/shard_map/all_gather | solution.py:89
  74.5 9.0 copy-start.7
  83.6 78.4 %copy-start.3 = (f32[32,128]{1,0:T(8,128)S(1)}, f32[32,128]{1,0:T(8,128)}, u32[]{:S(2)}) copy-start(f32[32,128]{1,0:T(8,128)} %param.22) | copy-start | bytes 49156
  83.6 86.5 %copy-start.4 = (f32[32,128]{1,0:T(8,128)S(1)}, f32[32,128]{1,0:T(8,128)}, u32[]{:S(2)}) copy-start(f32[32,128]{1,0:T(8,128)} %param.20) | copy-start | bytes 49156
  162.0 380.8 %all-gather.9.cloned.1.call-start = ((), (), s32[]{:S(2)}) async-start(), calls=%async_computation.2 | async-start | bytes 1310720 | tf_op jit(solution)/shard_map/all_gather | solution.py:105
  515.7 0.7 copy-start.1
  516.4 142.8 %all-gather.11.cloned.1.call-start = ((), (), s32[]{:S(2)}) async-start(), calls=%async_computation.3 | async-start | bytes 34603008 | tf_op jit(solution)/shard_map/all_gather | solution.py:19
  659.2 168.3 %copy-start.6 = (f32[512]{0:T(512)S(1)}, f32[512]{0:T(512)}, u32[]{:S(2)}) copy-start(f32[512]{0:T(512)} %param.23) | copy-start | bytes 6148
Sparse Core Ops, SparseCore 0:
  60.0 94.0 all-reduce.1
  162.1 157.6 all-gather.6
  516.5 26.1 all-gather.8
  545.1 114.0 all-gather.10
where the time goes:
time: 981 us; the launch traced here: 963 us
  matrix products  448 us (46%)
  waiting for transfers between devices  328 us (33%)
  local copies, waits for them, and re-layouts  126 us (13%)
  blocking collectives  39.5 us (4%)
  between operations  13.3 us (1%)
    all_gather x1, waiting for transfers between devices, body(): full_elements = lax.all_gather(element, 'state', axis=1, tiled=True)  138 us
    dot_general x96, matrix products, split_product(): jnp.dot(matrix, leading, preferred_element_type=jnp.float32)  126 us
    dot_general x96, matrix products, split_product(): jnp.dot(matrix, remainder, preferred_element_type=jnp.float32)  125 us
    dot_general x31, matrix products, combine(): jnp.dot(later[0], earlier[0], precision=HIGHEST)  95.1 us
    all_gather x1, waiting for transfers between devices, prefix(): pieces = jax.tree.map(lambda part: lax.all_gather(part, axis), value)  92.9 us
    psum x1, waiting for transfers between devices, body(): lax.psum(image_part.astype(jnp.bfloat16), 'state').astype(jnp.float32)  70.4 us
    dot_general x31, matrix products, combine(): jnp.dot(later[0], earlier[1], precision=HIGHEST) + later[1]  68.3 us
    dynamic_update_slice x32, local copies, waits for them, and re-layouts, body(): _, filtered = lax.scan(sweep, entry, (full_elements, full_offsets))  41.3 us
  transfers between devices with their start and end apart: 4, of which 4 were waited for; matrix products, arithmetic and copies ran while one was open for 3% of the time, Pallas kernels for 0%

commit v1 on v0

v1 whole, which is shorter than its diff:
```python
import jax
import jax.numpy as jnp
from jax import lax
from jax.experimental import pallas as pl
from jax.experimental.pallas import tpu as pltpu
from jax.sharding import PartitionSpec as P

MESH = pl.DeviceIdType.MESH
F32 = jnp.float32
BF16 = jnp.bfloat16
NS = 512
HALF = 256
STEPS = 8
CHUNK = 2
NCHUNK = STEPS // CHUNK


def split(value):
    high = value.astype(BF16)
    low = (value - high.astype(F32)).astype(BF16)
    return high, low


def column_to_row(column):
    rows = lax.broadcasted_iota(jnp.int32, (128, 128), 0)
    lanes = lax.broadcasted_iota(jnp.int32, (128, 128), 1)
    return jnp.sum(jnp.where(rows == lanes, column, 0.0), axis=0, keepdims=True)


def matvec(load, vector):
    out = []
    for g in range(4):
        total = load(g, 0) * vector[0]
        for j in range(1, 4):
            total = total + load(g, j) * vector[j]
        out.append(column_to_row(jnp.sum(total, axis=1, keepdims=True)))
    return out


def rows_of(ref):
    return [ref[g : g + 1, :] for g in range(4)]


def put_rows(ref, rows):
    for g in range(4):
        ref[g : g + 1, :] = rows[g]


def block_of_map(ref):
    def load(g, j):
        rows, lanes = pl.ds(g * 128, 128), pl.ds((j % 2) * 128, 128)
        return ref[j // 2, 0, rows, lanes].astype(F32) + ref[j // 2, 1, rows, lanes].astype(F32)

    return load


def block_of_plain(ref):
    def load(g, j):
        return ref[pl.ds(g * 128, 128), pl.ds(j * 128, 128)].astype(F32)

    return load


def product(left, right):
    total = None
    for h in range(2):
        rows = pl.ds(h * HALF, HALF)
        for a, b in ((0, 0), (0, 1), (1, 0)):
            term = jnp.dot(left[h, a], right[b, rows, :], preferred_element_type=F32)
            total = term if total is None else total + term
    return total


def to_plain(ref, out):
    for h in range(2):
        out[:, h * HALF : (h + 1) * HALF] = ref[h, 0].astype(F32) + ref[h, 1].astype(F32)


def kernel(
    columns_count,
    vals_ref, gain_ref, obs_op_ref, meta_ref, obs_values_ref, sources_ref, prior_ref,
    out_ref,
    packed, a_buf, b_buf, gain_buf, src_buf, meta_buf, meta_smem, op_buf, ov_buf,
    f_buf, fn_buf, e_buf, off_buf,
    maps, maps_q, chip, chip_q, partial, partial_q, before, before_q, whole,
    plain_a, plain_b, plain_c, x_in, x_out, x_work, sweep_buf,
    send_in, recv_in, send_small, recv_small, send_obs, recv_obs, smem_sem,
    send_map, recv_map, send_chip, recv_chip, send_y, recv_y, send_yq, recv_yq,
    send_left, recv_left, send_x, recv_x, send_out, recv_out, send_full, recv_full,
):
    tm, y = lax.axis_index("tm"), lax.axis_index("state")
    core = lax.rem(tm, 2)
    column = tm // 2
    first_tm = tm - core
    other = 1 - core
    sibling = (first_tm + other, y)
    last = columns_count - 1

    barrier = pltpu.get_barrier_semaphore()
    for c in range(2):
        for j in range(4):
            @pl.when(jnp.logical_or(c != core, j != y))
            def _():
                pl.semaphore_signal(barrier, inc=1, device_id=(first_tm + c, j), device_id_type=MESH)

    @pl.when(column > 0)
    def _():
        pl.semaphore_signal(barrier, inc=1, device_id=(tm - 2, 3), device_id_type=MESH)

    def pack(s, carry):
        left = vals_ref[s, 0, :, 128:192]
        right = vals_ref[s, 1, :, 128:192]
        packed[s] = jnp.concatenate([left, right], axis=1)
        return carry

    lax.fori_loop(0, 4 * STEPS, pack, 0)

    sends_on = jnp.logical_and(y == 3, column < last)

    @pl.when(sends_on)
    def _():
        pl.semaphore_wait(barrier, 11)

    @pl.when(jnp.logical_not(sends_on))
    def _():
        pl.semaphore_wait(barrier, 7)

    def target_of(b):
        return first_tm + b % 2, 2 * core + b // 2

    def is_me(b):
        dest_tm, dest_y = target_of(b)
        return jnp.logical_and(dest_tm == tm, dest_y == y)

    def remote(src, dst, send, recv, device):
        return pltpu.make_async_remote_copy(
            src_ref=src, dst_ref=dst, send_sem=send, recv_sem=recv, device_id=device, device_id_type=MESH
        )

    def small_pairs(b):
        start = pl.ds(8 * b, STEPS)
        return (
            (sources_ref.at[start], src_buf.at[y], 0),
            (meta_ref.at[start], meta_buf.at[y], 1),
        )

    def big_pairs(b, q):
        start, there = pl.ds(8 * b + CHUNK * q, CHUNK), pl.ds(CHUNK * q, CHUNK)
        return (
            (vals_ref.at[start, :, :, pl.ds(0, 128)], a_buf.at[y, there], 0),
            (packed.at[start], b_buf.at[y, there], 1),
            (gain_ref.at[start], gain_buf.at[y, there], 2),
        )

    def send_pair(b, src, dst, send, recv):
        @pl.when(jnp.logical_not(is_me(b)))
        def _():
            remote(src, dst, send, recv, target_of(b)).start()

        @pl.when(is_me(b))
        def _():
            pltpu.make_async_copy(src, dst, recv).start()

    for b in range(4):
        for src, dst, kind in small_pairs(b):
            send_pair(b, src, dst, send_small.at[b, kind], recv_small.at[y, kind])

    holds = core == y // 2
    mine_at = pl.ds(16 * lax.rem(y, 2) + 8 * core, STEPS)
    other_at = pl.ds(16 * lax.rem(y, 2) + 8 * other, STEPS)
    obs_arrays = ((obs_op_ref, op_buf, 0), (obs_values_ref, ov_buf, 1))

    @pl.when(holds)
    def _():
        for src, dst, kind in obs_arrays:
            remote(src.at[other_at], dst, send_obs.at[kind], recv_obs.at[kind], sibling).start()
            pltpu.make_async_copy(src.at[mine_at], dst, recv_obs.at[kind]).start()

    def start_chunk(q, carry):
        for b in range(4):
            for src, dst, kind in big_pairs(b, q):
                send_pair(b, src, dst, send_in.at[b, kind, q], recv_in.at[y, kind, q])
        return carry

    lax.fori_loop(0, NCHUNK, start_chunk, 0)

    def arrived(dst, sem):
        pltpu.make_async_copy(dst, dst, sem).wait()

    for j in range(4):
        arrived(src_buf.at[j], recv_small.at[j, 0])
        arrived(meta_buf.at[j], recv_small.at[j, 1])
    for src, dst, kind in obs_arrays:
        arrived(dst, recv_obs.at[kind])
    to_smem = pltpu.make_async_copy(meta_buf, meta_smem, smem_sem)
    to_smem.start()
    to_smem.wait()

    lane64 = lax.broadcasted_iota(jnp.int32, (64, 128), 1)
    row64 = lax.broadcasted_iota(jnp.int32, (64, 128), 0)
    left64 = lane64 < 64
    half64 = lane64 // 64
    lane1 = lax.broadcasted_iota(jnp.int32, (1, 128), 1)

    maps_q[core] = jnp.zeros((8, 128), F32)

    def step(s, carry):
        @pl.when(lax.rem(s, CHUNK) == 0)
        def _():
            q = s // CHUNK
            there = pl.ds(CHUNK * q, CHUNK)
            for j in range(4):
                arrived(a_buf.at[j, there], recv_in.at[j, 0, q])
                arrived(b_buf.at[j, there], recv_in.at[j, 1, q])
                arrived(gain_buf.at[j, there], recv_in.at[j, 2, q])

        for j in range(4):
            third = b_buf[j, s].astype(F32)
            third_turned = pltpu.roll(third, 64, 1)
            for il in range(2):
                i = 2 * j + il
                pair = a_buf[j, s, il].astype(F32)
                turned = pltpu.roll(pair, 64, 1)
                block0 = jnp.where(left64, pair, turned)
                block1 = jnp.where(left64, turned, pair)
                block2 = jnp.where(left64 if il == 0 else jnp.logical_not(left64), third, third_turned)
                col1 = meta_smem[j, s, 3 * il + 1]
                col2 = meta_smem[j, s, 3 * il + 2]
                for p in range(4):
                    index = half64 + 2 * p
                    value = jnp.where(index == col1, block1, jnp.where(index == col2, block2, 0.0))
                    if p == j:
                        value = jnp.where(half64 == il, block0, value)
                    f_buf[i, :, p * 128 : (p + 1) * 128] = value
                    fn_buf[i, :, p * 128 : (p + 1) * 128] = value.astype(BF16)

        operator = op_buf[s].astype(F32)
        turned_operator = operator.T.astype(BF16)
        count = meta_smem[0, s, 8]
        images, source_columns = [], []
        for o in range(2):
            block = meta_smem[0, s, 6 + o]
            selected = fn_buf[block]
            images.append(jnp.dot(turned_operator[64 * o : 64 * o + 64], selected, preferred_element_type=F32))
            source_row = src_buf[block // 2, pl.ds(s, 1), :]
            offset = lax.rem(block, 2) * 64
            source_columns.append(
                jnp.sum(jnp.where(lane64 == row64 + offset, source_row, 0.0), axis=1, keepdims=True)
            )
        image = jnp.concatenate(images, axis=0)
        slot = lax.broadcasted_iota(jnp.int32, (128, NS), 0)
        masked = jnp.where(slot < count, image, 0.0).astype(BF16)
        gains = gain_buf[:, s].reshape(NS, 128)
        correction = jnp.dot(gains, masked, preferred_element_type=F32)
        e_buf[s] = (f_buf[...].reshape(NS, NS) - correction).astype(BF16)

        source_image = jnp.sum(
            operator * jnp.where(left64, source_columns[0], source_columns[1]), axis=0, keepdims=True
        )
        source_image = source_image.astype(BF16).astype(F32)
        innovation = jnp.where(lane1 < count, ov_buf[pl.ds(s, 1), :] - source_image, 0.0)
        offsets = []
        for g in range(4):
            moved = jnp.sum(gain_buf[g, s].astype(F32) * innovation, axis=1, keepdims=True)
            offsets.append(column_to_row(moved) + src_buf[g, pl.ds(s, 1), :])
        put_rows(off_buf.at[s], offsets)

        moved = matvec(block_of_plain(e_buf.at[s]), rows_of(maps_q.at[core]))
        put_rows(maps_q.at[core], [m + o for m, o in zip(moved, offsets)])

        @pl.when(s == 0)
        def _():
            for h in range(2):
                maps[core, h, 0] = e_buf[s, :, h * HALF : (h + 1) * HALF]
                maps[core, h, 1] = jnp.zeros((NS, HALF), BF16)

        @pl.when(s > 0)
        def _():
            for h in range(2):
                matrix = e_buf[s]
                value = jnp.dot(matrix, maps[core, h, 0], preferred_element_type=F32)
                value = value + jnp.dot(matrix, maps[core, h, 1], preferred_element_type=F32)
                maps[core, h, 0], maps[core, h, 1] = split(value)

        return carry

    lax.fori_loop(0, STEPS, step, 0)

    map_copy = remote(maps.at[core], maps.at[core], send_map.at[0], recv_map.at[0], sibling)
    q_copy = remote(maps_q.at[core], maps_q.at[core], send_map.at[1], recv_map.at[1], sibling)
    map_copy.start()
    q_copy.start()
    arrived(maps_q.at[other], recv_map.at[1])
    arrived(maps.at[other], recv_map.at[0])
    chip[y, core, 0], chip[y, core, 1] = split(product(maps.at[1], maps.at[0, core]))
    moved = matvec(block_of_map(maps.at[1]), rows_of(maps_q.at[0]))
    put_rows(chip_q.at[y], [m + o for m, o in zip(moved, rows_of(maps_q.at[1]))])

    def y_copies(d):
        there = (tm, lax.rem(y + d, 4))
        return (
            remote(chip.at[y, core], chip.at[y, core], send_y.at[d], recv_y.at[y], there),
            remote(chip_q.at[y], chip_q.at[y], send_yq.at[d], recv_yq.at[y], there),
        )

    for d in (1, 2, 3):
        @pl.when(y + d <= 3)
        def _():
            for copy in y_copies(d):
                copy.start()

    own_copy = remote(chip.at[y, core], chip.at[y, core], send_chip, recv_chip, sibling)

    @pl.when(y == 3)
    def _():
        own_copy.start()

    to_plain(maps.at[0], plain_c)

    def left_copy(l):
        return remote(chip.at[l, core], chip.at[l, core], send_left.at[l], recv_left.at[l], sibling)

    for l in range(3):
        @pl.when(l < y)
        def _():
            arrived(chip_q.at[l], recv_yq.at[l])
    for l in (2, 1):
        @pl.when(l < y)
        def _():
            arrived(chip.at[l, core], recv_y.at[l])
            left_copy(l).start()

    @pl.when(y > 0)
    def _():
        arrived(chip.at[0, core], recv_y.at[0])
        partial[...] = chip[0, core]
        partial_q[...] = chip_q[0]

    def extend(l):
        high, low = split(product(chip.at[l], partial))
        partial[0], partial[1] = high, low
        moved = matvec(block_of_map(chip.at[l]), rows_of(partial_q))
        put_rows(partial_q, [m + o for m, o in zip(moved, rows_of(chip_q.at[l]))])

    for l in (1, 2):
        @pl.when(l < y)
        def _():
            arrived(chip.at[l, other], recv_left.at[l])
            extend(l)

    @pl.when(y > 0)
    def _():
        before[core] = partial[...]
        before_q[...] = partial_q[...]
        remote(before.at[core], before.at[core], send_full.at[0], recv_full.at[0], sibling).start()

    @pl.when(y == 3)
    def _():
        arrived(chip.at[y, other], recv_chip)
        extend(3)
        whole[core] = partial[...]
        copy = remote(whole.at[core], whole.at[core], send_full.at[1], recv_full.at[1], sibling)
        copy.start()
        arrived(whole.at[other], recv_full.at[1])
        to_plain(whole, plain_a)

    @pl.when(y > 0)
    def _():
        arrived(before.at[other], recv_full.at[0])
        to_plain(before, plain_b)

    def x_copy(j):
        return remote(x_out, x_in, send_x.at[j], recv_x, (tm + 2, j))

    @pl.when(column == 0)
    def _():
        x_in[...] = prior_ref[...]

    @pl.when(column > 0)
    def _():
        arrived(x_in, recv_x)

    @pl.when(jnp.logical_and(y == 3, column < last))
    def _():
        moved = matvec(block_of_plain(plain_a), rows_of(x_in))
        put_rows(x_out, [m + o for m, o in zip(moved, rows_of(partial_q))])
        for j in (3, 2, 1, 0):
            x_copy(j).start()

    @pl.when(y == 0)
    def _():
        x_work[...] = x_in[...]

    @pl.when(y > 0)
    def _():
        moved = matvec(block_of_plain(plain_b), rows_of(x_in))
        put_rows(x_work, [m + o for m, o in zip(moved, rows_of(before_q))])

    @pl.when(core == 1)
    def _():
        moved = matvec(block_of_plain(plain_c), rows_of(x_work))
        put_rows(x_work, [m + o for m, o in zip(moved, rows_of(maps_q.at[0]))])

    def sweep(s, carry):
        moved = matvec(block_of_plain(e_buf.at[s]), list(carry))
        rows = [m + o for m, o in zip(moved, rows_of(off_buf.at[s]))]
        for g in range(4):
            sweep_buf[g, pl.ds(s, 1), :] = rows[g]
        return tuple(rows)

    lax.fori_loop(0, STEPS, sweep, tuple(rows_of(x_work)))

    owner = first_tm + y // 2
    out_block = 2 * lax.rem(y, 2) + core
    here = pl.ds(8 * out_block, STEPS)

    def own_rows(g):
        return jnp.logical_and(owner == tm, g == y)

    for g in range(4):
        src, dst = sweep_buf.at[g], out_ref.at[here]

        @pl.when(jnp.logical_not(own_rows(g)))
        def _():
            remote(src, dst, send_out.at[g], recv_out.at[out_block], (owner, g)).start()

        @pl.when(own_rows(g))
        def _():
            pltpu.make_async_copy(src, dst, recv_out.at[out_block]).start()

    for b in range(4):
        arrived(out_ref.at[pl.ds(8 * b, STEPS)], recv_out.at[b])

    for g in range(4):
        @pl.when(jnp.logical_not(own_rows(g)))
        def _():
            remote(sweep_buf.at[g], out_ref.at[here], send_out.at[g], recv_out.at[out_block], (owner, g)).wait_send()

    for b in range(4):
        @pl.when(jnp.logical_not(is_me(b)))
        def _():
            for src, dst, kind in small_pairs(b):
                remote(src, dst, send_small.at[b, kind], recv_small.at[y, kind], target_of(b)).wait_send()

    def finish_chunk(q, carry):
        for b in range(4):
            @pl.when(jnp.logical_not(is_me(b)))
            def _():
                for src, dst, kind in big_pairs(b, q):
                    remote(src, dst, send_in.at[b, kind, q], recv_in.at[y, kind, q], target_of(b)).wait_send()
        return carry

    lax.fori_loop(0, NCHUNK, finish_chunk, 0)

    @pl.when(holds)
    def _():
        for src, dst, kind in obs_arrays:
            remote(src.at[other_at], dst, send_obs.at[kind], recv_obs.at[kind], sibling).wait_send()

    map_copy.wait_send()
    q_copy.wait_send()
    for d in (1, 2, 3):
        @pl.when(y + d <= 3)
        def _():
            for copy in y_copies(d):
                copy.wait_send()
    for l in (2, 1):
        @pl.when(l < y)
        def _():
            left_copy(l).wait_send()

    @pl.when(y > 0)
    def _():
        remote(before.at[core], before.at[core], send_full.at[0], recv_full.at[0], sibling).wait_send()

    @pl.when(y == 3)
    def _():
        own_copy.wait_send()
        remote(whole.at[core], whole.at[core], send_full.at[1], recv_full.at[1], sibling).wait_send()

    @pl.when(jnp.logical_and(y == 3, column < last))
    def _():
        for j in range(4):
            x_copy(j).wait_send()


def body(dyn_cols, dyn_vals, obs_blocks, obs_op, obs_counts, obs_values, gain, sources, prior):
    count = dyn_vals.shape[0]
    columns_count = lax.axis_size("tm") // 2
    meta = jnp.concatenate(
        [dyn_cols.reshape(count, 6), obs_blocks, obs_counts[:, None], jnp.zeros((count, 119), jnp.int32)], axis=1
    )
    prior_rows = jnp.concatenate([prior.reshape(4, 128), jnp.zeros((4, 128), F32)], axis=0)
    vmem = pl.BlockSpec(memory_space=pltpu.VMEM)
    hbm = pl.BlockSpec(memory_space=pl.ANY)
    dma = pltpu.SemaphoreType.DMA
    a_map = (2, 2, NS, HALF)

    def call(*refs):
        kernel(columns_count, *refs)

    return pl.pallas_call(
        call,
        out_shape=jax.ShapeDtypeStruct((count, 128), F32),
        in_specs=[vmem, hbm, vmem, vmem, vmem, vmem, vmem],
        out_specs=vmem,
        scratch_shapes=[
            pltpu.VMEM((count, 64, 128), BF16),
            pltpu.VMEM((4, STEPS, 2, 64, 128), BF16),
            pltpu.VMEM((4, STEPS, 64, 128), BF16),
            pltpu.VMEM((4, STEPS, 128, 128), BF16),
            pltpu.VMEM((4, STEPS, 128), F32),
            pltpu.VMEM((4, STEPS, 128), jnp.int32),
            pltpu.SMEM((4, STEPS, 128), jnp.int32),
            pltpu.VMEM((STEPS, 64, 128), BF16),
            pltpu.VMEM((STEPS, 128), F32),
            pltpu.VMEM((8, 64, NS), F32),
            pltpu.VMEM((8, 64, NS), BF16),
            pltpu.VMEM((STEPS, NS, NS), BF16),
            pltpu.VMEM((STEPS, 8, 128), F32),
            pltpu.VMEM((2, *a_map), BF16),
            pltpu.VMEM((2, 8, 128), F32),
            pltpu.VMEM((4, *a_map), BF16),
            pltpu.VMEM((4, 8, 128), F32),
            pltpu.VMEM((2, NS, HALF), BF16),
            pltpu.VMEM((8, 128), F32),
            pltpu.VMEM(a_map, BF16),
            pltpu.VMEM((8, 128), F32),
            pltpu.VMEM(a_map, BF16),
            pltpu.VMEM((NS, NS), F32),
            pltpu.VMEM((NS, NS), F32),
            pltpu.VMEM((NS, NS), F32),
            pltpu.VMEM((8, 128), F32),
            pltpu.VMEM((8, 128), F32),
            pltpu.VMEM((8, 128), F32),
            pltpu.VMEM((4, STEPS, 128), F32),
            dma((4, 3, NCHUNK)), dma((4, 3, NCHUNK)),
            dma((4, 2)), dma((4, 2)),
            dma((2,)), dma((2,)), dma,
            dma((2,)), dma((2,)),
            dma, dma,
            dma((4,)), dma((4,)), dma((4,)), dma((4,)),
            dma((4,)), dma((4,)),
            dma((4,)), dma,
            dma((4,)), dma((4,)),
            dma((2,)), dma((2,)),
        ],
        compiler_params=pltpu.CompilerParams(
            collective_id=0, has_side_effects=True, vmem_limit_bytes=58 * 1024 * 1024
        ),
        cost_estimate=pl.CostEstimate(flops=10_000_000_000, bytes_accessed=4_000_000, transcendentals=0),
    )(dyn_vals, gain, obs_op, meta, obs_values, sources, prior_rows)


def solution(mesh):
    return jax.shard_map(
        body,
        mesh=mesh,
        in_specs=(
            P("tm", "state", None),
            P("tm", "state", None, None),
            P("tm", None),
            P("tm", None, None),
            P("tm"),
            P("tm", None),
            P("tm", "state", None),
            P("tm", "state"),
            P(),
        ),
        out_specs=P("tm", "state"),
        check_vma=False,
    )
```

time: 981 us -> 127 us (0.13); the launches traced: 963 us -> 126 us
  matrix products: 448 us -> 0 us
  waiting for transfers between devices: 328 us -> 0 us
  local copies, waits for them, and re-layouts: 126 us -> 4.95 us
  Pallas kernels: 0 us -> 121 us
  blocking collectives: 39.5 us -> 0 us
  between operations: 13.3 us -> 0.01 us
    dot_general x262 -> x0, matrix products: 448 us -> none  [the longest x96 126 us: split_product(): jnp.dot(matrix, leading, preferred_element_type=jnp.float32)]
    all_gather x3 -> x0, waiting for transfers between devices: 258 us -> none  [the longest x1 138 us: body(): full_elements = lax.all_gather(element, 'state', axis=1, tiled=True)]
    pallas_call x0 -> x1, Pallas kernels: none -> 121 us  [body(): pl.pallas_call(call, out_shape=jax.ShapeDtypeStruct((count, 128), F32), i...]
    psum x1 -> x0, waiting for transfers between devices: 70.4 us -> none  [body(): lax.psum(image_part.astype(jnp.bfloat16), 'state').astype(jnp.float32)]
    dynamic_update_slice x32 -> x0, local copies, waits for them, and re-layouts: 41.3 us -> none  [body(): _, filtered = lax.scan(sweep, entry, (full_elements, full_offsets))]
    all_gather x2 -> x0, blocking collectives: 32.9 us -> none  [the longest x1 23.3 us: prefix(): pieces = jax.tree.map(lambda part: lax.all_gather(part, axis), value)]
    unnamed x23 -> x3, local copies, waits for them, and re-layouts: 28.1 us -> 2.77 us
    another operation x2 -> x0, local copies, waits for them, and re-layouts: 23.6 us -> none  [body(): forward.reshape(step_count, local_rows, NS) - correction]
  transfers between devices with their start and end apart: 4 -> 0, of which waited for: 4 -> 0; matrix products, arithmetic and copies ran while one was open for 3% -> 0% of each run, Pallas kernels for 0% -> 0%
where the time goes in v1:
time: 127 us; the launch traced here: 126 us
  Pallas kernels  121 us (95%)
  local copies, waits for them, and re-layouts  4.95 us (4%)
    pallas_call x1, Pallas kernels, body(): pl.pallas_call(call, out_shape=jax.ShapeDtypeStruct((count, 128), F32), i...  121 us
    unnamed x3, local copies, waits for them, and re-layouts  2.77 us

profile of v1, /device:TPU:103, one launch (start us, length us, event | category | flops | bytes accessed | tf_op | source)
XLA Modules:
  0.0 126.5 jit_solution(4128197812102476418)
XLA Ops:
  0.0 0.7 copy.13
  0.7 0.1 copy.14
  0.8 0.8 copy.15
  1.5 0.7 copy.16
  2.3 0.1 pad.4.clone
  2.4 0.7 add_add_fusion.refs_3_
  3.0 1.3 %concatenate.7.refs_6_ = f32[8,128]{1,0:T(8,128)} pad(f32[4,128]{1,0:T(4,128)} %bitcast.4, f32[]{:T(128)} %constant.1.clone.1), padding=0_4x0_0 | pad | bytes 6148 | tf_op jit(solution)/shard_map/concatenate | solution.py:493
  4.3 120.8 %shard_map.91 = f32[32,128]{1,0:T(8,128)} custom-call(bf16[32,2,64,192]{3,2,1,0:T(8,128)(2,1)} %refs_0_.1, bf16[32,128,128]{2,1,0:T(8,128)(2,1)} %refs_1_.1, bf16[32,64,128]{2,1,0:T(8,128)(2,1)} %refs_2_.1, s32[32,128]{1,0:T(8,128)} %add_add_fusion.refs_3_, f32[32,128]{1,0:T(8,128)} %refs_4_.1, f32[32,128]{1,0:T(8,128)} %refs_5_.1, f32[8,128]{1,0:T(8,128)} %concatenate.7.refs_6_), custom_call_target="tpu_custom_call" | custom-call | flops 10000000000 | bytes 4000000 | tf_op jit(solution)/shard_map/pallas_call | solution.py:502
  125.1 1.3 %copy.18 = f32[32,128]{1,0:T(8,128)} copy(f32[32,128]{1,0:T(8,128)} %shard_map.91) | data formatting | bytes 32768
  (2 shorter events, 0.0 us)

commit v2 on v1

--- a/solution.py
+++ b/solution.py
@@ -78,15 +78,17 @@
 
 def kernel(
     columns_count,
-    vals_ref, gain_ref, obs_op_ref, meta_ref, obs_values_ref, sources_ref, prior_ref,
+    vals_ref, gain_ref, obs_op_ref, cols_ref, blocks_ref, counts_ref, obs_values_ref, sources_ref, prior_ref,
     out_ref,
-    packed, a_buf, b_buf, gain_buf, src_buf, meta_buf, meta_smem, op_buf, ov_buf,
+    third, packed, a_buf, b_buf, gain_buf, src_buf, cols_buf, blocks_buf, counts_buf,
+    cols_smem, blocks_smem, counts_smem, op_buf, ov_buf,
     f_buf, fn_buf, e_buf, off_buf,
     maps, maps_q, chip, chip_q, partial, partial_q, before, before_q, whole,
-    plain_a, plain_b, plain_c, x_in, x_out, x_work, sweep_buf,
+    mate, mate_q, plain_a, plain_b, plain_c, plain_d, x_in, x_pair, x_mid, x_out, x_work, sweep_buf,
     send_in, recv_in, send_small, recv_small, send_obs, recv_obs, smem_sem,
     send_map, recv_map, send_chip, recv_chip, send_y, recv_y, send_yq, recv_yq,
     send_left, recv_left, send_x, recv_x, send_out, recv_out, send_full, recv_full,
+    third_sem, send_mate, recv_mate, recv_pair,
 ):
     tm, y = lax.axis_index("tm"), lax.axis_index("state")
     core = lax.rem(tm, 2)
@@ -94,36 +96,67 @@
     first_tm = tm - core
     other = 1 - core
     sibling = (first_tm + other, y)
-    last = columns_count - 1
+    pair, second = column // 2, lax.rem(column, 2)
+    even_pair = lax.rem(pair, 2) == 0
+    last_pair = columns_count // 2 - 1
+
+    def master_column(p):
+        return 2 * p + 1 - lax.rem(p, 2)
+
+    def device(c, j):
+        return 2 * c + core, j
+
+    in_master = column == master_column(pair)
+    is_master = jnp.logical_and(in_master, y == 3)
+    is_mate = jnp.logical_and(jnp.logical_not(in_master), y == 3)
+    partner = device(column + 1 - 2 * second, 3)
 
     barrier = pltpu.get_barrier_semaphore()
+
+    def greet(where):
+        pl.semaphore_signal(barrier, inc=1, device_id=where, device_id_type=MESH)
+
     for c in range(2):
         for j in range(4):
             @pl.when(jnp.logical_or(c != core, j != y))
             def _():
-                pl.semaphore_signal(barrier, inc=1, device_id=(first_tm + c, j), device_id_type=MESH)
-
-    @pl.when(column > 0)
-    def _():
-        pl.semaphore_signal(barrier, inc=1, device_id=(tm - 2, 3), device_id_type=MESH)
-
-    def pack(s, carry):
-        left = vals_ref[s, 0, :, 128:192]
-        right = vals_ref[s, 1, :, 128:192]
-        packed[s] = jnp.concatenate([left, right], axis=1)
-        return carry
-
-    lax.fori_loop(0, 4 * STEPS, pack, 0)
-
-    sends_on = jnp.logical_and(y == 3, column < last)
-
-    @pl.when(sends_on)
-    def _():
-        pl.semaphore_wait(barrier, 11)
-
-    @pl.when(jnp.logical_not(sends_on))
-    def _():
-        pl.semaphore_wait(barrier, 7)
+                greet((first_tm + c, j))
+
+    third_copy = pltpu.make_async_copy(vals_ref.at[:, :, :, pl.ds(128, 64)], third, third_sem)
+    third_copy.start()
+
+    from_earlier = jnp.logical_and(second == 0, pair > 0)
+    from_own = jnp.logical_and(second == 1, jnp.logical_not(even_pair))
+    earlier_master = device(master_column(pair - 1), 3)
+
+    @pl.when(from_earlier)
+    def _():
+        greet(earlier_master)
+
+    @pl.when(from_own)
+    def _():
+        greet(device(column - 1, 3))
+
+    takes_pair = jnp.logical_and(is_master, jnp.logical_and(even_pair, pair > 0))
+
+    @pl.when(takes_pair)
+    def _():
+        greet(earlier_master)
+
+    @pl.when(is_master)
+    def _():
+        greet(partner)
+
+    sends_on = jnp.logical_and(is_master, pair < last_pair)
+    odd_master = jnp.logical_and(is_master, jnp.logical_not(even_pair))
+    peers = (
+        7
+        + jnp.where(is_mate, 1, 0)
+        + jnp.where(odd_master, 4, 0)
+        + jnp.where(sends_on, 4, 0)
+        + jnp.where(jnp.logical_and(sends_on, odd_master), 1, 0)
+    )
+    pl.semaphore_wait(barrier, peers)
 
     def target_of(b):
         return first_tm + b % 2, 2 * core + b // 2
@@ -141,15 +174,15 @@
         start = pl.ds(8 * b, STEPS)
         return (
             (sources_ref.at[start], src_buf.at[y], 0),
-            (meta_ref.at[start], meta_buf.at[y], 1),
+            (cols_ref, cols_buf.at[y], 1),
         )
 
     def big_pairs(b, q):
         start, there = pl.ds(8 * b + CHUNK * q, CHUNK), pl.ds(CHUNK * q, CHUNK)
         return (
             (vals_ref.at[start, :, :, pl.ds(0, 128)], a_buf.at[y, there], 0),
+            (gain_ref.at[start], gain_buf.at[y, there], 2),
             (packed.at[start], b_buf.at[y, there], 1),
-            (gain_ref.at[start], gain_buf.at[y, there], 2),
         )
 
     def send_pair(b, src, dst, send, recv):
@@ -166,20 +199,38 @@
             send_pair(b, src, dst, send_small.at[b, kind], recv_small.at[y, kind])
 
     holds = core == y // 2
-    mine_at = pl.ds(16 * lax.rem(y, 2) + 8 * core, STEPS)
+    first_step = 16 * lax.rem(y, 2) + 8 * core
+    mine_at = pl.ds(first_step, STEPS)
     other_at = pl.ds(16 * lax.rem(y, 2) + 8 * other, STEPS)
-    obs_arrays = ((obs_op_ref, op_buf, 0), (obs_values_ref, ov_buf, 1))
+    obs_arrays = (
+        (obs_op_ref.at[mine_at], obs_op_ref.at[other_at], op_buf, 0),
+        (obs_values_ref.at[mine_at], obs_values_ref.at[other_at], ov_buf, 1),
+        (blocks_ref, blocks_ref, blocks_buf, 2),
+        (counts_ref, counts_ref, counts_buf, 3),
+    )
 
     @pl.when(holds)
     def _():
-        for src, dst, kind in obs_arrays:
-            remote(src.at[other_at], dst, send_obs.at[kind], recv_obs.at[kind], sibling).start()
-            pltpu.make_async_copy(src.at[mine_at], dst, recv_obs.at[kind]).start()
+        for mine, others, dst, kind in obs_arrays:
+            remote(others, dst, send_obs.at[kind], recv_obs.at[kind], sibling).start()
+            pltpu.make_async_copy(mine, dst, recv_obs.at[kind]).start()
 
     def start_chunk(q, carry):
         for b in range(4):
-            for src, dst, kind in big_pairs(b, q):
+            for src, dst, kind in big_pairs(b, q)[:2]:
                 send_pair(b, src, dst, send_in.at[b, kind, q], recv_in.at[y, kind, q])
+
+        @pl.when(q == 0)
+        def _():
+            third_copy.wait()
+
+        for b in range(4):
+            for t in range(CHUNK):
+                at = 8 * b + CHUNK * q + t
+                packed[at] = jnp.concatenate([third[at, 0], third[at, 1]], axis=1)
+        for b in range(4):
+            src, dst, kind = big_pairs(b, q)[2]
+            send_pair(b, src, dst, send_in.at[b, kind, q], recv_in.at[y, kind, q])
         return carry
 
     lax.fori_loop(0, NCHUNK, start_chunk, 0)
@@ -189,12 +240,17 @@
 
     for j in range(4):
         arrived(src_buf.at[j], recv_small.at[j, 0])
-        arrived(meta_buf.at[j], recv_small.at[j, 1])
-    for src, dst, kind in obs_arrays:
+        arrived(cols_buf.at[j], recv_small.at[j, 1])
+    for _, _, dst, kind in obs_arrays:
         arrived(dst, recv_obs.at[kind])
-    to_smem = pltpu.make_async_copy(meta_buf, meta_smem, smem_sem)
-    to_smem.start()
-    to_smem.wait()
+    to_smem = [
+        pltpu.make_async_copy(src, dst, smem_sem.at[k])
+        for k, (src, dst) in enumerate(((cols_buf, cols_smem), (blocks_buf, blocks_smem), (counts_buf, counts_smem)))
+    ]
+    for copy in to_smem:
+        copy.start()
+    for copy in to_smem:
+        copy.wait()
 
     lane64 = lax.broadcasted_iota(jnp.int32, (64, 128), 1)
     row64 = lax.broadcasted_iota(jnp.int32, (64, 128), 0)
@@ -202,9 +258,11 @@
     half64 = lane64 // 64
     lane1 = lax.broadcasted_iota(jnp.int32, (1, 128), 1)
 
-    maps_q[core] = jnp.zeros((8, 128), F32)
+    maps_q[core] = jnp.zeros((4, 128), F32)
 
     def step(s, carry):
+        at = first_step + s
+
         @pl.when(lax.rem(s, CHUNK) == 0)
         def _():
             q = s // CHUNK
@@ -215,17 +273,17 @@
                 arrived(gain_buf.at[j, there], recv_in.at[j, 2, q])
 
         for j in range(4):
-            third = b_buf[j, s].astype(F32)
-            third_turned = pltpu.roll(third, 64, 1)
+            thirds = b_buf[j, s].astype(F32)
+            thirds_turned = pltpu.roll(thirds, 64, 1)
             for il in range(2):
                 i = 2 * j + il
                 pair = a_buf[j, s, il].astype(F32)
                 turned = pltpu.roll(pair, 64, 1)
                 block0 = jnp.where(left64, pair, turned)
                 block1 = jnp.where(left64, turned, pair)
-                block2 = jnp.where(left64 if il == 0 else jnp.logical_not(left64), third, third_turned)
-                col1 = meta_smem[j, s, 3 * il + 1]
-                col2 = meta_smem[j, s, 3 * il + 2]
+                block2 = jnp.where(left64 if il == 0 else jnp.logical_not(left64), thirds, thirds_turned)
+                col1 = cols_smem[j, 1, il, at]
+                col2 = cols_smem[j, 2, il, at]
                 for p in range(4):
                     index = half64 + 2 * p
                     value = jnp.where(index == col1, block1, jnp.where(index == col2, block2, 0.0))
@@ -236,10 +294,10 @@
 
         operator = op_buf[s].astype(F32)
         turned_operator = operator.T.astype(BF16)
-        count = meta_smem[0, s, 8]
+        count = counts_smem[0, at]
         images, source_columns = [], []
         for o in range(2):
-            block = meta_smem[0, s, 6 + o]
+            block = blocks_smem[o, at]
             selected = fn_buf[block]
             images.append(jnp.dot(turned_operator[64 * o : 64 * o + 64], selected, preferred_element_type=F32))
             source_row = src_buf[block // 2, pl.ds(s, 1), :]
@@ -354,38 +412,100 @@
         before_q[...] = partial_q[...]
         remote(before.at[core], before.at[core], send_full.at[0], recv_full.at[0], sibling).start()
 
+    mate_copy = remote(partial, mate.at[core], send_mate.at[0], recv_mate.at[0], partner)
+    mate_q_copy = remote(partial_q, mate_q, send_mate.at[1], recv_mate.at[1], partner)
+    mate_on = remote(mate.at[core], mate.at[core], send_mate.at[2], recv_mate.at[2], sibling)
+
     @pl.when(y == 3)
     def _():
         arrived(chip.at[y, other], recv_chip)
         extend(3)
+
+    @pl.when(is_mate)
+    def _():
+        mate_copy.start()
+        mate_q_copy.start()
+
+    @pl.when(is_master)
+    def _():
         whole[core] = partial[...]
         copy = remote(whole.at[core], whole.at[core], send_full.at[1], recv_full.at[1], sibling)
         copy.start()
+        arrived(mate.at[core], recv_mate.at[0])
+        mate_on.start()
         arrived(whole.at[other], recv_full.at[1])
         to_plain(whole, plain_a)
+        arrived(mate_q, recv_mate.at[1])
+        arrived(mate.at[other], recv_mate.at[2])
+        to_plain(mate, plain_d)
 
     @pl.when(y > 0)
     def _():
         arrived(before.at[other], recv_full.at[0])
         to_plain(before, plain_b)
 
-    def x_copy(j):
-        return remote(x_out, x_in, send_x.at[j], recv_x, (tm + 2, j))
-
-    @pl.when(column == 0)
+    def next_pair_copy():
+        return remote(x_out, x_pair, send_x.at[8], recv_pair, device(master_column(pair + 1), 3))
+
+    def next_copy(j):
+        return remote(x_out, x_in, send_x.at[j], recv_x, device(2 * pair + 2, j))
+
+    def second_copy(j):
+        return remote(x_mid, x_in, send_x.at[4 + j], recv_x, device(2 * pair + 1, j))
+
+    def apply(plain, vector, shift, out):
+        moved = matvec(block_of_plain(plain), rows_of(vector))
+        put_rows(out, [m + o for m, o in zip(moved, rows_of(shift))])
+
+    @pl.when(jnp.logical_and(pair == 0, second == 0))
     def _():
         x_in[...] = prior_ref[...]
 
-    @pl.when(column > 0)
+    @pl.when(jnp.logical_or(from_earlier, from_own))
     def _():
         arrived(x_in, recv_x)
 
-    @pl.when(jnp.logical_and(y == 3, column < last))
-    def _():
-        moved = matvec(block_of_plain(plain_a), rows_of(x_in))
-        put_rows(x_out, [m + o for m, o in zip(moved, rows_of(partial_q))])
-        for j in (3, 2, 1, 0):
-            x_copy(j).start()
+    @pl.when(is_master)
+    def _():
+        @pl.when(even_pair)
+        def _():
+            @pl.when(pair == 0)
+            def _():
+                x_pair[...] = prior_ref[...]
+
+            @pl.when(pair > 0)
+            def _():
+                arrived(x_pair, recv_pair)
+
+            apply(plain_d, x_pair, mate_q, x_mid)
+            apply(plain_a, x_mid, partial_q, x_out)
+
+            @pl.when(sends_on)
+            def _():
+                for j in (3, 2, 1, 0):
+                    next_copy(j).start()
+
+            for j in range(3):
+                second_copy(j).start()
+            x_in[...] = x_mid[...]
+
+        @pl.when(jnp.logical_not(even_pair))
+        def _():
+            apply(plain_a, x_in, partial_q, x_mid)
+            apply(plain_d, x_mid, mate_q, x_out)
+
+            @pl.when(sends_on)
+            def _():
+                next_pair_copy().start()
+                for j in range(4):
+                    next_copy(j).start()
+
+            for j in range(4):
+                second_copy(j).start()
+
+    @pl.when(jnp.logical_and(jnp.logical_and(even_pair, second == 1), y < 3))
+    def _():
+        arrived(x_in, recv_x)
 
     @pl.when(y == 0)
     def _():
@@ -454,8 +574,8 @@
 
     @pl.when(holds)
     def _():
-        for src, dst, kind in obs_arrays:
-            remote(src.at[other_at], dst, send_obs.at[kind], recv_obs.at[kind], sibling).wait_send()
+        for mine, others, dst, kind in obs_arrays:
+            remote(others, dst, send_obs.at[kind], recv_obs.at[kind], sibling).wait_send()
 
     map_copy.wait_send()
     q_copy.wait_send()
@@ -476,21 +596,40 @@
     @pl.when(y == 3)
     def _():
         own_copy.wait_send()
+
+    @pl.when(is_mate)
+    def _():
+        mate_copy.wait_send()
+        mate_q_copy.wait_send()
+
+    @pl.when(is_master)
+    def _():
         remote(whole.at[core], whole.at[core], send_full.at[1], recv_full.at[1], sibling).wait_send()
-
-    @pl.when(jnp.logical_and(y == 3, column < last))
+        mate_on.wait_send()
+        for j in range(3):
+            second_copy(j).wait_send()
+
+    @pl.when(odd_master)
+    def _():
+        second_copy(3).wait_send()
+
+    @pl.when(sends_on)
     def _():
         for j in range(4):
-            x_copy(j).wait_send()
+            next_copy(j).wait_send()
+
+    @pl.when(jnp.logical_and(sends_on, odd_master))
+    def _():
+        next_pair_copy().wait_send()
 
 
 def body(dyn_cols, dyn_vals, obs_blocks, obs_op, obs_counts, obs_values, gain, sources, prior):
     count = dyn_vals.shape[0]
     columns_count = lax.axis_size("tm") // 2
-    meta = jnp.concatenate(
-        [dyn_cols.reshape(count, 6), obs_blocks, obs_counts[:, None], jnp.zeros((count, 119), jnp.int32)], axis=1
-    )
-    prior_rows = jnp.concatenate([prior.reshape(4, 128), jnp.zeros((4, 128), F32)], axis=0)
+    cols = jnp.transpose(dyn_cols, (2, 1, 0))
+    blocks = jnp.transpose(obs_blocks, (1, 0))
+    counts = obs_counts.reshape(1, count)
+    prior_rows = prior.reshape(4, 128)
     vmem = pl.BlockSpec(memory_space=pltpu.VMEM)
     hbm = pl.BlockSpec(memory_space=pl.ANY)
     dma = pltpu.SemaphoreType.DMA
@@ -502,54 +641,65 @@
     return pl.pallas_call(
         call,
         out_shape=jax.ShapeDtypeStruct((count, 128), F32),
-        in_specs=[vmem, hbm, vmem, vmem, vmem, vmem, vmem],
+        in_specs=[hbm, hbm, hbm, vmem, vmem, vmem, vmem, vmem, vmem],
         out_specs=vmem,
         scratch_shapes=[
+            pltpu.VMEM((count, 2, 64, 64), BF16),
             pltpu.VMEM((count, 64, 128), BF16),
             pltpu.VMEM((4, STEPS, 2, 64, 128), BF16),
             pltpu.VMEM((4, STEPS, 64, 128), BF16),
             pltpu.VMEM((4, STEPS, 128, 128), BF16),
             pltpu.VMEM((4, STEPS, 128), F32),
-            pltpu.VMEM((4, STEPS, 128), jnp.int32),
-            pltpu.SMEM((4, STEPS, 128), jnp.int32),
+            pltpu.VMEM((4, *cols.shape), jnp.int32),
+            pltpu.VMEM(blocks.shape, jnp.int32),
+            pltpu.VMEM(counts.shape, jnp.int32),
+            pltpu.SMEM((4, *cols.shape), jnp.int32),
+            pltpu.SMEM(blocks.shape, jnp.int32),
+            pltpu.SMEM(counts.shape, jnp.int32),
             pltpu.VMEM((STEPS, 64, 128), BF16),
             pltpu.VMEM((STEPS, 128), F32),
             pltpu.VMEM((8, 64, NS), F32),
             pltpu.VMEM((8, 64, NS), BF16),
             pltpu.VMEM((STEPS, NS, NS), BF16),
-            pltpu.VMEM((STEPS, 8, 128), F32),
+            pltpu.VMEM((STEPS, 4, 128), F32),
             pltpu.VMEM((2, *a_map), BF16),
-            pltpu.VMEM((2, 8, 128), F32),
+            pltpu.VMEM((2, 4, 128), F32),
             pltpu.VMEM((4, *a_map), BF16),
-            pltpu.VMEM((4, 8, 128), F32),
+            pltpu.VMEM((4, 4, 128), F32),
             pltpu.VMEM((2, NS, HALF), BF16),
-            pltpu.VMEM((8, 128), F32),
+            pltpu.VMEM((4, 128), F32),
             pltpu.VMEM(a_map, BF16),
-            pltpu.VMEM((8, 128), F32),
+            pltpu.VMEM((4, 128), F32),
             pltpu.VMEM(a_map, BF16),
+            pltpu.VMEM(a_map, BF16),
+            pltpu.VMEM((4, 128), F32),
             pltpu.VMEM((NS, NS), F32),
             pltpu.VMEM((NS, NS), F32),
             pltpu.VMEM((NS, NS), F32),
-            pltpu.VMEM((8, 128), F32),
-            pltpu.VMEM((8, 128), F32),
-            pltpu.VMEM((8, 128), F32),
+            pltpu.VMEM((NS, NS), F32),
+            pltpu.VMEM((4, 128), F32),
+            pltpu.VMEM((4, 128), F32),
+            pltpu.VMEM((4, 128), F32),
+            pltpu.VMEM((4, 128), F32),
+            pltpu.VMEM((4, 128), F32),
             pltpu.VMEM((4, STEPS, 128), F32),
             dma((4, 3, NCHUNK)), dma((4, 3, NCHUNK)),
             dma((4, 2)), dma((4, 2)),
-            dma((2,)), dma((2,)), dma,
+            dma((4,)), dma((4,)), dma((3,)),
             dma((2,)), dma((2,)),
             dma, dma,
             dma((4,)), dma((4,)), dma((4,)), dma((4,)),
             dma((4,)), dma((4,)),
-            dma((4,)), dma,
+            dma((9,)), dma,
             dma((4,)), dma((4,)),
             dma((2,)), dma((2,)),
+            dma, dma((3,)), dma((3,)), dma,
         ],
         compiler_params=pltpu.CompilerParams(
             collective_id=0, has_side_effects=True, vmem_limit_bytes=58 * 1024 * 1024
         ),
         cost_estimate=pl.CostEstimate(flops=10_000_000_000, bytes_accessed=4_000_000, transcendentals=0),
-    )(dyn_vals, gain, obs_op, meta, obs_values, sources, prior_rows)
+    )(dyn_vals, gain, obs_op, cols, blocks, counts, obs_values, sources, prior_rows)
 
 
 def solution(mesh):

time: 127 us -> 116 us (0.913)
  Pallas kernels: 121 us -> 114 us
  local copies, waits for them, and re-layouts: 4.95 us -> 1.32 us
    pallas_call x1, Pallas kernels: 121 us -> 114 us  [body(): pl.pallas_call(call, out_shape=jax.ShapeDtypeStruct((count, 128), F32), i...]
    unnamed x3 -> x1, local copies, waits for them, and re-layouts: 2.77 us -> 1.32 us
    concatenate x2 -> x0, local copies, waits for them, and re-layouts: 1.35 us -> none  [the longest x1 1.27 us: body(): jnp.concatenate([prior.reshape(4, 128), jnp.zeros((4, 128), F32)], axis=0)]
where the time goes in v2:
time: 116 us
  Pallas kernels  114 us (98%)
  local copies, waits for them, and re-layouts  1.32 us (1%)
    pallas_call x1, Pallas kernels, body(): pl.pallas_call(call, out_shape=jax.ShapeDtypeStruct((count, 128), F32), i...  114 us

profile of v2, /device:TPU:103, one launch (start us, length us, event | category | flops | bytes accessed | tf_op | source)
XLA Modules:
  0.0 115.6 jit_solution(1126077724781836813)
XLA Ops:
  0.0 114.3 %shard_map.91 = f32[32,128]{1,0:T(8,128)} custom-call(bf16[32,2,64,192]{3,2,1,0:T(8,128)(2,1)} %refs_0_.1, bf16[32,128,128]{2,1,0:T(8,128)(2,1)} %refs_1_.1, bf16[32,64,128]{2,1,0:T(8,128)(2,1)} %refs_2_.1, s32[3,2,32]{2,1,0:T(2,128)} %bitcast.4, s32[2,32]{1,0:T(2,128)} %bitcast.6, s32[1,32]{1,0:T(1,128)} %bitcast.7, f32[32,128]{1,0:T(8,128)} %refs_6_.1, ...), custom_call_target="tpu_custom_call" | custom-call | flops 10000000000 | bytes 4000000 | tf_op jit(solution)/shard_map/pallas_call | solution.py:641
  114.3 1.3 %copy.11 = f32[32,128]{1,0:T(8,128)} copy(f32[32,128]{1,0:T(8,128)} %shard_map.91) | data formatting | bytes 32768

commit v3 on v2

--- a/solution.py
+++ b/solution.py
@@ -46,14 +46,6 @@
         ref[g : g + 1, :] = rows[g]
 
 
-def block_of_map(ref):
-    def load(g, j):
-        rows, lanes = pl.ds(g * 128, 128), pl.ds((j % 2) * 128, 128)
-        return ref[j // 2, 0, rows, lanes].astype(F32) + ref[j // 2, 1, rows, lanes].astype(F32)
-
-    return load
-
-
 def block_of_plain(ref):
     def load(g, j):
         return ref[pl.ds(g * 128, 128), pl.ds(j * 128, 128)].astype(F32)
@@ -71,9 +63,58 @@
     return total
 
 
-def to_plain(ref, out):
+def half_map(maps_ref, out):
     for h in range(2):
-        out[:, h * HALF : (h + 1) * HALF] = ref[h, 0].astype(F32) + ref[h, 1].astype(F32)
+        out[:, h * HALF : (h + 1) * HALF] = maps_ref[h, 0].astype(F32) + maps_ref[h, 1].astype(F32)
+
+
+def left_lanes(shape):
+    return lax.broadcasted_iota(jnp.int32, shape, 1) < 64
+
+
+def pack_chunk(doubled):
+    low = doubled - doubled.astype(BF16).astype(F32)
+    return jnp.where(left_lanes(doubled.shape), doubled, low).astype(BF16)
+
+
+def pack_pair(pair):
+    turned = pltpu.roll(pair, 64, 1)
+    left = left_lanes(pair.shape)
+    return pack_chunk(jnp.where(left, pair, turned)), pack_chunk(jnp.where(left, turned, pair))
+
+
+def chunk_product(left, right):
+    rows = right.reshape(8, 64, 128)
+    rows = jnp.concatenate([rows, rows], axis=1).reshape(2 * NS, 128)
+    lanes = jnp.concatenate([left[n] for n in range(8)], axis=1)
+    parts = jnp.dot(lanes, rows, preferred_element_type=F32)
+    return pack_chunk(parts + pltpu.roll(parts, 64, 1))
+
+
+def to_plain(packed, out):
+    for n in range(4):
+        first, second = packed[2 * n].astype(F32), packed[2 * n + 1].astype(F32)
+        first, second = first + pltpu.roll(first, 64, 1), second + pltpu.roll(second, 64, 1)
+        out[:, n * 128 : (n + 1) * 128] = jnp.where(left_lanes(first.shape), first, second)
+
+
+def packed_matvec(packed, vector):
+    doubled = []
+    for row in vector:
+        doubled.append(jnp.concatenate([row[:, :64], row[:, :64]], axis=1))
+        doubled.append(jnp.concatenate([row[:, 64:], row[:, 64:]], axis=1))
+    out = []
+    for g in range(4):
+        total = None
+        for n in range(8):
+            term = packed[n, pl.ds(g * 128, 128), :].astype(F32) * doubled[n]
+            total = term if total is None else total + term
+        out.append(column_to_row(jnp.sum(total, axis=1, keepdims=True)))
+    return out
+
+
+def sum_rows(a, b):
+    return [m + o for m, o in zip(a, b)]
 
 
 def kernel(
@@ -83,12 +124,12 @@
     third, packed, a_buf, b_buf, gain_buf, src_buf, cols_buf, blocks_buf, counts_buf,
     cols_smem, blocks_smem, counts_smem, op_buf, ov_buf,
     f_buf, fn_buf, e_buf, off_buf,
-    maps, maps_q, chip, chip_q, partial, partial_q, before, before_q, whole,
+    maps, maps_q, chip, chip_q, before, before_q, left, left_q, first, first_q, last, whole, whole_q,
     mate, mate_q, plain_a, plain_b, plain_c, plain_d, x_in, x_pair, x_mid, x_out, x_work, sweep_buf,
     send_in, recv_in, send_small, recv_small, send_obs, recv_obs, smem_sem,
-    send_map, recv_map, send_chip, recv_chip, send_y, recv_y, send_yq, recv_yq,
-    send_left, recv_left, send_x, recv_x, send_out, recv_out, send_full, recv_full,
-    third_sem, send_mate, recv_mate, recv_pair,
+    send_map, recv_map, send_before, recv_before, send_left, recv_left, send_first, recv_first,
+    send_mate, recv_mate, send_vec, recv_vec, send_share, recv_share, send_on, recv_on,
+    send_x, recv_x, recv_pair, send_out, recv_out, third_sem,
 ):
     tm, y = lax.axis_index("tm"), lax.axis_index("state")
     core = lax.rem(tm, 2)
@@ -350,99 +391,176 @@
     q_copy.start()
     arrived(maps_q.at[other], recv_map.at[1])
     arrived(maps.at[other], recv_map.at[0])
-    chip[y, core, 0], chip[y, core, 1] = split(product(maps.at[1], maps.at[0, core]))
-    moved = matvec(block_of_map(maps.at[1]), rows_of(maps_q.at[0]))
-    put_rows(chip_q.at[y], [m + o for m, o in zip(moved, rows_of(maps_q.at[1]))])
-
-    def y_copies(d):
-        there = (tm, lax.rem(y + d, 4))
-        return (
-            remote(chip.at[y, core], chip.at[y, core], send_y.at[d], recv_y.at[y], there),
-            remote(chip_q.at[y], chip_q.at[y], send_yq.at[d], recv_yq.at[y], there),
-        )
-
-    for d in (1, 2, 3):
-        @pl.when(y + d <= 3)
-        def _():
-            for copy in y_copies(d):
-                copy.start()
-
-    own_copy = remote(chip.at[y, core], chip.at[y, core], send_chip, recv_chip, sibling)
+    for h in range(2):
+        total = product(maps.at[1], maps.at[0, core, :, :, pl.ds(128 * h, 128)])
+        chip[4 * core + 2 * h], chip[4 * core + 2 * h + 1] = pack_pair(total)
+
+    mine = pl.ds(4 * core, 4)
+    theirs = pl.ds(4 * other, 4)
+
+    def to_chip(j):
+        return tm, j
+
+    def share(ref, k):
+        return remote(ref.at[mine], ref.at[mine], send_share.at[k], recv_share.at[k], sibling)
+
+    def shared(ref, k):
+        arrived(ref.at[theirs], recv_share.at[k])
+
+    def chip_before_copy(k):
+        n = 4 * core + k
+        return remote(chip.at[n], before.at[n], send_before.at[k], recv_before.at[k], to_chip(1))
+
+    def chip_left_copy(k):
+        n = 4 * core + k
+        return remote(chip.at[n], left.at[n], send_left.at[k], recv_left.at[k], to_chip(3))
+
+    def first_copy(k):
+        return remote(first.at[k], first.at[k], send_first.at[k], recv_first.at[k], to_chip(3))
+
+    first_before_copy = remote(first, before.at[mine], send_before.at[4], recv_before.at[4], to_chip(2))
+
+    def mate_copy(k):
+        n = 4 * core + k
+        return remote(whole.at[n], mate.at[n], send_mate.at[k], recv_mate.at[k], partner)
+
+    def mate_on(k):
+        n = 4 * core + k
+        return remote(mate.at[n], mate.at[n], send_on.at[k], recv_on.at[k], sibling)
+
+    vec_copies = (
+        remote(chip_q, before_q, send_vec.at[0], recv_vec.at[0], to_chip(1)),
+        remote(chip_q, left_q, send_vec.at[1], recv_vec.at[1], to_chip(3)),
+        remote(first_q, first_q, send_vec.at[2], recv_vec.at[2], to_chip(3)),
+        remote(first_q, before_q, send_vec.at[3], recv_vec.at[0], to_chip(2)),
+        remote(whole_q, mate_q, send_vec.at[4], recv_vec.at[3], partner),
+    )
+
+    def chunks(step):
+        def one(k, carry):
+            step(k)
+            return carry
+
+        lax.fori_loop(0, 4, one, 0)
+
+    @pl.when(y == 0)
+    def _():
+        chunks(lambda k: chip_before_copy(k).start())
+
+    @pl.when(y == 2)
+    def _():
+        chunks(lambda k: chip_left_copy(k).start())
+
+    @pl.when(lax.rem(y, 2) == 1)
+    def _():
+        share(chip, 0).start()
+
+    half_map(maps.at[0], plain_c)
+    half_map(maps.at[1], plain_b)
+    moved = matvec(block_of_plain(plain_b), rows_of(maps_q.at[0]))
+    put_rows(chip_q, sum_rows(moved, rows_of(maps_q.at[1])))
+
+    @pl.when(y == 0)
+    def _():
+        vec_copies[0].start()
+
+    @pl.when(y == 2)
+    def _():
+        vec_copies[1].start()
+
+    @pl.when(lax.rem(y, 2) == 1)
+    def _():
+        shared(chip, 0)
+
+    @pl.when(y == 1)
+    def _():
+        def one(k):
+            n = 4 * core + k
+            arrived(before.at[n], recv_before.at[k])
+            first[k] = chunk_product(chip, before[n])
+            first_copy(k).start()
+
+        chunks(one)
+        first_before_copy.start()
+        share(before, 1).start()
+        arrived(before_q, recv_vec.at[0])
+        put_rows(first_q, sum_rows(packed_matvec(chip, rows_of(before_q)), rows_of(chip_q)))
+        vec_copies[2].start()
+        vec_copies[3].start()
+
+    @pl.when(y == 2)
+    def _():
+        arrived(before.at[mine], recv_before.at[4])
+        share(before, 1).start()
+        arrived(before_q, recv_vec.at[0])
 
     @pl.when(y == 3)
     def _():
-        own_copy.start()
-
-    to_plain(maps.at[0], plain_c)
-
-    def left_copy(l):
-        return remote(chip.at[l, core], chip.at[l, core], send_left.at[l], recv_left.at[l], sibling)
-
-    for l in range(3):
-        @pl.when(l < y)
-        def _():
-            arrived(chip_q.at[l], recv_yq.at[l])
-    for l in (2, 1):
-        @pl.when(l < y)
-        def _():
-            arrived(chip.at[l, core], recv_y.at[l])
-            left_copy(l).start()
+        def one_last(k):
+            n = 4 * core + k
+            arrived(left.at[n], recv_left.at[k])
+            last[n] = chunk_product(chip, left[n])
+
+        chunks(one_last)
+        share(last, 2).start()
+        share(left, 3).start()
+        arrived(left_q, recv_vec.at[1])
+        put_rows(whole_q, sum_rows(packed_matvec(chip, rows_of(left_q)), rows_of(chip_q)))
+        shared(last, 2)
+
+        def one_whole(k):
+            n = 4 * core + k
+            arrived(first.at[k], recv_first.at[k])
+            whole[n] = chunk_product(last, first[k])
+
+            @pl.when(is_mate)
+            def _():
+                mate_copy(k).start()
+
+        chunks(one_whole)
+
+        @pl.when(is_master)
+        def _():
+            share(whole, 4).start()
+
+        arrived(first_q, recv_vec.at[2])
+        put_rows(whole_q, sum_rows(packed_matvec(last, rows_of(first_q)), rows_of(whole_q)))
+
+        @pl.when(is_mate)
+        def _():
+            vec_copies[4].start()
+
+        shared(left, 3)
+
+        def one_before(k):
+            before[4 * core + k] = chunk_product(left, first[k])
+
+        chunks(one_before)
+        share(before, 1).start()
+        put_rows(before_q, sum_rows(packed_matvec(left, rows_of(first_q)), rows_of(left_q)))
+
+    @pl.when(is_master)
+    def _():
+        shared(whole, 4)
+        to_plain(whole, plain_a)
+
+        def one_mate(k):
+            arrived(mate.at[4 * core + k], recv_mate.at[k])
+            mate_on(k).start()
+
+        chunks(one_mate)
 
     @pl.when(y > 0)
     def _():
-        arrived(chip.at[0, core], recv_y.at[0])
-        partial[...] = chip[0, core]
-        partial_q[...] = chip_q[0]
-
-    def extend(l):
-        high, low = split(product(chip.at[l], partial))
-        partial[0], partial[1] = high, low
-        moved = matvec(block_of_map(chip.at[l]), rows_of(partial_q))
-        put_rows(partial_q, [m + o for m, o in zip(moved, rows_of(chip_q.at[l]))])
-
-    for l in (1, 2):
-        @pl.when(l < y)
-        def _():
-            arrived(chip.at[l, other], recv_left.at[l])
-            extend(l)
-
-    @pl.when(y > 0)
-    def _():
-        before[core] = partial[...]
-        before_q[...] = partial_q[...]
-        remote(before.at[core], before.at[core], send_full.at[0], recv_full.at[0], sibling).start()
-
-    mate_copy = remote(partial, mate.at[core], send_mate.at[0], recv_mate.at[0], partner)
-    mate_q_copy = remote(partial_q, mate_q, send_mate.at[1], recv_mate.at[1], partner)
-    mate_on = remote(mate.at[core], mate.at[core], send_mate.at[2], recv_mate.at[2], sibling)
-
-    @pl.when(y == 3)
-    def _():
-        arrived(chip.at[y, other], recv_chip)
-        extend(3)
-
-    @pl.when(is_mate)
-    def _():
-        mate_copy.start()
-        mate_q_copy.start()
+        shared(before, 1)
+        to_plain(before, plain_b)
 
     @pl.when(is_master)
     def _():
-        whole[core] = partial[...]
-        copy = remote(whole.at[core], whole.at[core], send_full.at[1], recv_full.at[1], sibling)
-        copy.start()
-        arrived(mate.at[core], recv_mate.at[0])
-        mate_on.start()
-        arrived(whole.at[other], recv_full.at[1])
-        to_plain(whole, plain_a)
-        arrived(mate_q, recv_mate.at[1])
-        arrived(mate.at[other], recv_mate.at[2])
+        arrived(mate_q, recv_vec.at[3])
+        for k in range(4):
+            arrived(mate.at[4 * other + k], recv_on.at[k])
         to_plain(mate, plain_d)
-
-    @pl.when(y > 0)
-    def _():
-        arrived(before.at[other], recv_full.at[0])
-        to_plain(before, plain_b)
 
     def next_pair_copy():
         return remote(x_out, x_pair, send_x.at[8], recv_pair, device(master_column(pair + 1), 3))
@@ -478,7 +596,7 @@
                 arrived(x_pair, recv_pair)
 
             apply(plain_d, x_pair, mate_q, x_mid)
-            apply(plain_a, x_mid, partial_q, x_out)
+            apply(plain_a, x_mid, whole_q, x_out)
 
             @pl.when(sends_on)
             def _():
@@ -491,7 +609,7 @@
 
         @pl.when(jnp.logical_not(even_pair))
         def _():
-            apply(plain_a, x_in, partial_q, x_mid)
+            apply(plain_a, x_in, whole_q, x_mid)
             apply(plain_d, x_mid, mate_q, x_out)
 
             @pl.when(sends_on)
@@ -579,33 +697,46 @@
 
     map_copy.wait_send()
     q_copy.wait_send()
-    for d in (1, 2, 3):
-        @pl.when(y + d <= 3)
-        def _():
-            for copy in y_copies(d):
-                copy.wait_send()
-    for l in (2, 1):
-        @pl.when(l < y)
-        def _():
-            left_copy(l).wait_send()
+
+    @pl.when(y == 0)
+    def _():
+        chunks(lambda k: chip_before_copy(k).wait_send())
+        vec_copies[0].wait_send()
+
+    @pl.when(y == 1)
+    def _():
+        chunks(lambda k: first_copy(k).wait_send())
+        first_before_copy.wait_send()
+        vec_copies[2].wait_send()
+        vec_copies[3].wait_send()
+
+    @pl.when(y == 2)
+    def _():
+        chunks(lambda k: chip_left_copy(k).wait_send())
+        vec_copies[1].wait_send()
+
+    @pl.when(lax.rem(y, 2) == 1)
+    def _():
+        share(chip, 0).wait_send()
 
     @pl.when(y > 0)
     def _():
-        remote(before.at[core], before.at[core], send_full.at[0], recv_full.at[0], sibling).wait_send()
+        share(before, 1).wait_send()
 
     @pl.when(y == 3)
     def _():
-        own_copy.wait_send()
+        share(last, 2).wait_send()
+        share(left, 3).wait_send()
 
     @pl.when(is_mate)
     def _():
-        mate_copy.wait_send()
-        mate_q_copy.wait_send()
+        chunks(lambda k: mate_copy(k).wait_send())
+        vec_copies[4].wait_send()
 
     @pl.when(is_master)
     def _():
-        remote(whole.at[core], whole.at[core], send_full.at[1], recv_full.at[1], sibling).wait_send()
-        mate_on.wait_send()
+        share(whole, 4).wait_send()
+        chunks(lambda k: mate_on(k).wait_send())
         for j in range(3):
             second_copy(j).wait_send()
 
@@ -634,6 +765,7 @@
     hbm = pl.BlockSpec(memory_space=pl.ANY)
     dma = pltpu.SemaphoreType.DMA
     a_map = (2, 2, NS, HALF)
+    packed_map = (8, NS, 128)
 
     def call(*refs):
         kernel(columns_count, *refs)
@@ -664,14 +796,18 @@
             pltpu.VMEM((STEPS, 4, 128), F32),
             pltpu.VMEM((2, *a_map), BF16),
             pltpu.VMEM((2, 4, 128), F32),
-            pltpu.VMEM((4, *a_map), BF16),
-            pltpu.VMEM((4, 4, 128), F32),
-            pltpu.VMEM((2, NS, HALF), BF16),
-            pltpu.VMEM((4, 128), F32),
-            pltpu.VMEM(a_map, BF16),
-            pltpu.VMEM((4, 128), F32),
-            pltpu.VMEM(a_map, BF16),
-            pltpu.VMEM(a_map, BF16),
+            pltpu.VMEM(packed_map, BF16),
+            pltpu.VMEM((4, 128), F32),
+            pltpu.VMEM(packed_map, BF16),
+            pltpu.VMEM((4, 128), F32),
+            pltpu.VMEM(packed_map, BF16),
+            pltpu.VMEM((4, 128), F32),
+            pltpu.VMEM((4, NS, 128), BF16),
+            pltpu.VMEM((4, 128), F32),
+            pltpu.VMEM(packed_map, BF16),
+            pltpu.VMEM(packed_map, BF16),
+            pltpu.VMEM((4, 128), F32),
+            pltpu.VMEM(packed_map, BF16),
             pltpu.VMEM((4, 128), F32),
             pltpu.VMEM((NS, NS), F32),
             pltpu.VMEM((NS, NS), F32),
@@ -686,14 +822,9 @@
             dma((4, 3, NCHUNK)), dma((4, 3, NCHUNK)),
             dma((4, 2)), dma((4, 2)),
             dma((4,)), dma((4,)), dma((3,)),
-            dma((2,)), dma((2,)),
-            dma, dma,
-            dma((4,)), dma((4,)), dma((4,)), dma((4,)),
-            dma((4,)), dma((4,)),
-            dma((9,)), dma,
-            dma((4,)), dma((4,)),
-            dma((2,)), dma((2,)),
-            dma, dma((3,)), dma((3,)), dma,
+            dma((2,)), dma((2,)), dma((5,)), dma((5,)), dma((4,)), dma((4,)), dma((4,)), dma((4,)),
+            dma((4,)), dma((4,)), dma((5,)), dma((4,)), dma((5,)), dma((5,)), dma((4,)), dma((4,)),
+            dma((9,)), dma, dma, dma((4,)), dma((4,)), dma,
         ],
         compiler_params=pltpu.CompilerParams(
             collective_id=0, has_side_effects=True, vmem_limit_bytes=58 * 1024 * 1024

time: 116 us -> 101 us (0.87)
  Pallas kernels: 114 us -> 100 us
    pallas_call x1, Pallas kernels: 114 us -> 100 us  [body(): pl.pallas_call(call, out_shape=jax.ShapeDtypeStruct((count, 128), F32), i...]
where the time goes in v3:
time: 101 us
  Pallas kernels  100 us (99%)
  local copies, waits for them, and re-layouts  1.32 us (1%)
    pallas_call x1, Pallas kernels, body(): pl.pallas_call(call, out_shape=jax.ShapeDtypeStruct((count, 128), F32), i...  100 us

profile of v3, /device:TPU:103, one launch (start us, length us, event | category | flops | bytes accessed | tf_op | source)
XLA Modules:
  0.0 101.3 jit_solution(8499493771201254829)
XLA Ops:
  0.0 100.0 %shard_map.91 = f32[32,128]{1,0:T(8,128)} custom-call(bf16[32,2,64,192]{3,2,1,0:T(8,128)(2,1)} %refs_0_.1, bf16[32,128,128]{2,1,0:T(8,128)(2,1)} %refs_1_.1, bf16[32,64,128]{2,1,0:T(8,128)(2,1)} %refs_2_.1, s32[3,2,32]{2,1,0:T(2,128)} %bitcast.4, s32[2,32]{1,0:T(2,128)} %bitcast.6, s32[1,32]{1,0:T(1,128)} %bitcast.7, f32[32,128]{1,0:T(8,128)} %refs_6_.1, ...), custom_call_target="tpu_custom_call" | custom-call | flops 10000000000 | bytes 4000000 | tf_op jit(solution)/shard_map/pallas_call | solution.py:773
  100.0 1.3 %copy.11 = f32[32,128]{1,0:T(8,128)} copy(f32[32,128]{1,0:T(8,128)} %shard_map.91) | data formatting | bytes 32768

commit v4 on v3

--- a/solution.py
+++ b/solution.py
@@ -125,11 +125,11 @@
     cols_smem, blocks_smem, counts_smem, op_buf, ov_buf,
     f_buf, fn_buf, e_buf, off_buf,
     maps, maps_q, chip, chip_q, before, before_q, left, left_q, first, first_q, last, whole, whole_q,
-    mate, mate_q, plain_a, plain_b, plain_c, plain_d, x_in, x_pair, x_mid, x_out, x_work, sweep_buf,
+    mate, mate_q, plain_a, plain_b, plain_c, plain_d, plain_e, x_in, x_pair, x_mid, x_out, x_end, x_work, sweep_buf,
     send_in, recv_in, send_small, recv_small, send_obs, recv_obs, smem_sem,
     send_map, recv_map, send_before, recv_before, send_left, recv_left, send_first, recv_first,
     send_mate, recv_mate, send_vec, recv_vec, send_share, recv_share, send_on, recv_on,
-    send_x, recv_x, recv_pair, send_out, recv_out, third_sem,
+    send_x, recv_x, recv_pair, send_out, recv_out, third_sem, send_end,
 ):
     tm, y = lax.axis_index("tm"), lax.axis_index("state")
     core = lax.rem(tm, 2)
@@ -147,10 +147,21 @@
     def device(c, j):
         return 2 * c + core, j
 
-    in_master = column == master_column(pair)
-    is_master = jnp.logical_and(in_master, y == 3)
-    is_mate = jnp.logical_and(jnp.logical_not(in_master), y == 3)
-    partner = device(column + 1 - 2 * second, 3)
+    single = column < 4
+    last_row = column >= columns_count - 4
+    end_column = columns_count - 1
+    in_master = jnp.where(last_row, column == columns_count - 3, column == master_column(pair))
+    at_last_chip = jnp.logical_and(y == 3, jnp.logical_not(single))
+    single_master = jnp.logical_and(y == 3, single)
+    is_master = jnp.logical_and(at_last_chip, in_master)
+    is_mate = jnp.logical_and(
+        at_last_chip, jnp.logical_and(jnp.logical_not(in_master), column != end_column)
+    )
+    end_master = jnp.logical_and(is_master, last_row)
+    end_mate = jnp.logical_and(is_mate, column == columns_count - 2)
+    partner = device(jnp.where(last_row, columns_count - 3, column + 1 - 2 * second), 3)
+    mate_column = column + 1 - 2 * second
+    mate_slot = jnp.where(column == columns_count - 2, 1, 0)
 
     barrier = pltpu.get_barrier_semaphore()
 
@@ -166,9 +177,14 @@
     third_copy = pltpu.make_async_copy(vals_ref.at[:, :, :, pl.ds(128, 64)], third, third_sem)
     third_copy.start()
 
-    from_earlier = jnp.logical_and(second == 0, pair > 0)
-    from_own = jnp.logical_and(second == 1, jnp.logical_not(even_pair))
-    earlier_master = device(master_column(pair - 1), 3)
+    from_single = jnp.logical_and(column > 0, column <= 4)
+    from_earlier = jnp.logical_and(second == 0, pair > 2)
+    from_own = jnp.logical_and(second == 1, jnp.logical_not(jnp.logical_or(even_pair, single)))
+    earlier_master = device(jnp.where(pair == 2, 3, master_column(pair - 1)), 3)
+
+    @pl.when(from_single)
+    def _():
+        greet(device(column - 1, 3))
 
     @pl.when(from_earlier)
     def _():
@@ -176,26 +192,31 @@
 
     @pl.when(from_own)
     def _():
-        greet(device(column - 1, 3))
-
-    takes_pair = jnp.logical_and(is_master, jnp.logical_and(even_pair, pair > 0))
-
-    @pl.when(takes_pair)
+        greet(device(jnp.where(last_row, columns_count - 3, column - 1), 3))
+
+    even_master = jnp.logical_and(is_master, even_pair)
+    odd_master = jnp.logical_and(is_master, jnp.logical_not(even_pair))
+
+    @pl.when(even_master)
     def _():
         greet(earlier_master)
 
     @pl.when(is_master)
     def _():
-        greet(partner)
-
-    sends_on = jnp.logical_and(is_master, pair < last_pair)
-    odd_master = jnp.logical_and(is_master, jnp.logical_not(even_pair))
+        greet(device(mate_column, 3))
+
+    @pl.when(end_master)
+    def _():
+        greet(device(column + 1, 3))
+
+    sends_pair = jnp.logical_or(jnp.logical_and(single_master, column == 3), odd_master)
     peers = (
         7
+        + jnp.where(jnp.logical_or(single_master, is_master), 4, 0)
         + jnp.where(is_mate, 1, 0)
         + jnp.where(odd_master, 4, 0)
-        + jnp.where(sends_on, 4, 0)
-        + jnp.where(jnp.logical_and(sends_on, odd_master), 1, 0)
+        + jnp.where(end_master, 4, 0)
+        + jnp.where(sends_pair, 1, 0)
     )
     pl.semaphore_wait(barrier, peers)
 
@@ -422,18 +443,18 @@
 
     def mate_copy(k):
         n = 4 * core + k
-        return remote(whole.at[n], mate.at[n], send_mate.at[k], recv_mate.at[k], partner)
-
-    def mate_on(k):
+        return remote(whole.at[n], mate.at[mate_slot, n], send_mate.at[k], recv_mate.at[mate_slot, k], partner)
+
+    def mate_on(k, slot):
         n = 4 * core + k
-        return remote(mate.at[n], mate.at[n], send_on.at[k], recv_on.at[k], sibling)
+        return remote(mate.at[slot, n], mate.at[slot, n], send_on.at[slot, k], recv_on.at[slot, k], sibling)
 
     vec_copies = (
         remote(chip_q, before_q, send_vec.at[0], recv_vec.at[0], to_chip(1)),
         remote(chip_q, left_q, send_vec.at[1], recv_vec.at[1], to_chip(3)),
         remote(first_q, first_q, send_vec.at[2], recv_vec.at[2], to_chip(3)),
         remote(first_q, before_q, send_vec.at[3], recv_vec.at[0], to_chip(2)),
-        remote(whole_q, mate_q, send_vec.at[4], recv_vec.at[3], partner),
+        remote(whole_q, mate_q.at[mate_slot], send_vec.at[4], recv_vec.at[3 + mate_slot], partner),
     )
 
     def chunks(step):
@@ -519,7 +540,7 @@
 
         chunks(one_whole)
 
-        @pl.when(is_master)
+        @pl.when(jnp.logical_or(is_master, single_master))
         def _():
             share(whole, 4).start()
 
@@ -530,6 +551,48 @@
         def _():
             vec_copies[4].start()
 
+    def entry():
+        @pl.when(column == 0)
+        def _():
+            x_in[...] = prior_ref[...]
+
+        @pl.when(jnp.logical_or(from_single, jnp.logical_or(from_earlier, from_own)))
+        def _():
+            arrived(x_in, recv_x)
+
+    def apply(plain, vector, shift, out):
+        moved = matvec(block_of_plain(plain), rows_of(vector))
+        put_rows(out, [m + o for m, o in zip(moved, rows_of(shift))])
+
+    def next_pair_copy():
+        there = jnp.where(single, 5, master_column(pair + 1))
+        return remote(x_out, x_pair, send_x.at[8], recv_pair, device(there, 3))
+
+    def next_copy(j):
+        return remote(x_out, x_in, send_x.at[j], recv_x, device(jnp.where(single, column + 1, 2 * pair + 2), j))
+
+    def second_copy(j):
+        return remote(x_mid, x_in, send_x.at[4 + j], recv_x, device(2 * pair + 1, j))
+
+    def end_copy(j):
+        return remote(x_end, x_in, send_end.at[j], recv_x, device(end_column, j))
+
+    @pl.when(single_master)
+    def _():
+        shared(whole, 4)
+        to_plain(whole, plain_a)
+        entry()
+        apply(plain_a, x_in, whole_q, x_out)
+
+        @pl.when(sends_pair)
+        def _():
+            next_pair_copy().start()
+
+        for j in (3, 2, 1, 0):
+            next_copy(j).start()
+
+    @pl.when(y == 3)
+    def _():
         shared(left, 3)
 
         def one_before(k):
@@ -544,84 +607,73 @@
         shared(whole, 4)
         to_plain(whole, plain_a)
 
-        def one_mate(k):
-            arrived(mate.at[4 * core + k], recv_mate.at[k])
-            mate_on(k).start()
-
-        chunks(one_mate)
+        def one_mate(slot):
+            def one(k):
+                arrived(mate.at[slot, 4 * core + k], recv_mate.at[slot, k])
+                mate_on(k, slot).start()
+
+            chunks(one)
+
+        one_mate(0)
+
+        @pl.when(last_row)
+        def _():
+            one_mate(1)
 
     @pl.when(y > 0)
     def _():
         shared(before, 1)
         to_plain(before, plain_b)
 
-    @pl.when(is_master)
-    def _():
-        arrived(mate_q, recv_vec.at[3])
+    def take_mate(slot, plain):
+        arrived(mate_q.at[slot], recv_vec.at[3 + slot])
         for k in range(4):
-            arrived(mate.at[4 * other + k], recv_on.at[k])
-        to_plain(mate, plain_d)
-
-    def next_pair_copy():
-        return remote(x_out, x_pair, send_x.at[8], recv_pair, device(master_column(pair + 1), 3))
-
-    def next_copy(j):
-        return remote(x_out, x_in, send_x.at[j], recv_x, device(2 * pair + 2, j))
-
-    def second_copy(j):
-        return remote(x_mid, x_in, send_x.at[4 + j], recv_x, device(2 * pair + 1, j))
-
-    def apply(plain, vector, shift, out):
-        moved = matvec(block_of_plain(plain), rows_of(vector))
-        put_rows(out, [m + o for m, o in zip(moved, rows_of(shift))])
-
-    @pl.when(jnp.logical_and(pair == 0, second == 0))
-    def _():
-        x_in[...] = prior_ref[...]
-
-    @pl.when(jnp.logical_or(from_earlier, from_own))
-    def _():
-        arrived(x_in, recv_x)
-
-    @pl.when(is_master)
-    def _():
-        @pl.when(even_pair)
-        def _():
-            @pl.when(pair == 0)
+            arrived(mate.at[slot, 4 * other + k], recv_on.at[slot, k])
+        to_plain(mate.at[slot], plain)
+
+    @pl.when(jnp.logical_not(single_master))
+    def _():
+        @pl.when(is_master)
+        def _():
+            take_mate(0, plain_d)
+
+            @pl.when(last_row)
             def _():
-                x_pair[...] = prior_ref[...]
-
-            @pl.when(pair > 0)
-            def _():
-                arrived(x_pair, recv_pair)
-
-            apply(plain_d, x_pair, mate_q, x_mid)
-            apply(plain_a, x_mid, whole_q, x_out)
-
-            @pl.when(sends_on)
-            def _():
-                for j in (3, 2, 1, 0):
-                    next_copy(j).start()
-
-            for j in range(3):
-                second_copy(j).start()
-            x_in[...] = x_mid[...]
-
-        @pl.when(jnp.logical_not(even_pair))
-        def _():
-            apply(plain_a, x_in, whole_q, x_mid)
-            apply(plain_d, x_mid, mate_q, x_out)
-
-            @pl.when(sends_on)
-            def _():
-                next_pair_copy().start()
-                for j in range(4):
-                    next_copy(j).start()
-
+                take_mate(1, plain_e)
+
+        entry()
+
+    @pl.when(even_master)
+    def _():
+        arrived(x_pair, recv_pair)
+        apply(plain_d, x_pair, mate_q.at[0], x_mid)
+        apply(plain_a, x_mid, whole_q, x_out)
+
+        @pl.when(last_row)
+        def _():
+            apply(plain_e, x_out, mate_q.at[1], x_end)
             for j in range(4):
-                second_copy(j).start()
-
-    @pl.when(jnp.logical_and(jnp.logical_and(even_pair, second == 1), y < 3))
+                end_copy(j).start()
+
+        for j in (3, 2, 1, 0):
+            next_copy(j).start()
+        for j in range(3):
+            second_copy(j).start()
+        x_in[...] = x_mid[...]
+
+    @pl.when(odd_master)
+    def _():
+        apply(plain_a, x_in, whole_q, x_mid)
+        apply(plain_d, x_mid, mate_q.at[0], x_out)
+        next_pair_copy().start()
+        for j in range(4):
+            next_copy(j).start()
+        for j in range(4):
+            second_copy(j).start()
+
+    waits_own = jnp.logical_and(jnp.logical_and(even_pair, second == 1), y < 3)
+
+    @pl.when(jnp.logical_and(waits_own, jnp.logical_not(single)))
     def _():
         arrived(x_in, recv_x)
 
@@ -733,23 +785,29 @@
         chunks(lambda k: mate_copy(k).wait_send())
         vec_copies[4].wait_send()
 
+    @pl.when(jnp.logical_or(is_master, single_master))
+    def _():
+        share(whole, 4).wait_send()
+        for j in range(4):
+            next_copy(j).wait_send()
+
     @pl.when(is_master)
     def _():
-        share(whole, 4).wait_send()
-        chunks(lambda k: mate_on(k).wait_send())
+        chunks(lambda k: mate_on(k, 0).wait_send())
         for j in range(3):
             second_copy(j).wait_send()
 
+    @pl.when(end_master)
+    def _():
+        chunks(lambda k: mate_on(k, 1).wait_send())
+        for j in range(4):
+            end_copy(j).wait_send()
+
     @pl.when(odd_master)
     def _():
         second_copy(3).wait_send()
 
-    @pl.when(sends_on)
-    def _():
-        for j in range(4):
-            next_copy(j).wait_send()
-
-    @pl.when(jnp.logical_and(sends_on, odd_master))
+    @pl.when(sends_pair)
     def _():
         next_pair_copy().wait_send()
 
@@ -807,12 +865,14 @@
             pltpu.VMEM(packed_map, BF16),
             pltpu.VMEM(packed_map, BF16),
             pltpu.VMEM((4, 128), F32),
-            pltpu.VMEM(packed_map, BF16),
-            pltpu.VMEM((4, 128), F32),
+            pltpu.VMEM((2, *packed_map), BF16),
+            pltpu.VMEM((2, 4, 128), F32),
             pltpu.VMEM((NS, NS), F32),
             pltpu.VMEM((NS, NS), F32),
             pltpu.VMEM((NS, NS), F32),
             pltpu.VMEM((NS, NS), F32),
+            pltpu.VMEM((NS, NS), F32),
+            pltpu.VMEM((4, 128), F32),
             pltpu.VMEM((4, 128), F32),
             pltpu.VMEM((4, 128), F32),
             pltpu.VMEM((4, 128), F32),
@@ -823,8 +883,8 @@
             dma((4, 2)), dma((4, 2)),
             dma((4,)), dma((4,)), dma((3,)),
             dma((2,)), dma((2,)), dma((5,)), dma((5,)), dma((4,)), dma((4,)), dma((4,)), dma((4,)),
-            dma((4,)), dma((4,)), dma((5,)), dma((4,)), dma((5,)), dma((5,)), dma((4,)), dma((4,)),
-            dma((9,)), dma, dma, dma((4,)), dma((4,)), dma,
+            dma((4,)), dma((2, 4)), dma((5,)), dma((5,)), dma((5,)), dma((5,)), dma((2, 4)), dma((2, 4)),
+            dma((9,)), dma, dma, dma((4,)), dma((4,)), dma, dma((4,)),
         ],
         compiler_params=pltpu.CompilerParams(
             collective_id=0, has_side_effects=True, vmem_limit_bytes=58 * 1024 * 1024

time: 101 us -> 98.1 us (0.971)
  Pallas kernels: 100 us -> 96.5 us
    pallas_call x1, Pallas kernels: 100 us -> 96.5 us  [body(): pl.pallas_call(call, out_shape=jax.ShapeDtypeStruct((count, 128), F32), i...]
where the time goes in v4:
time: 98.1 us; the launch traced here: 97.8 us
  Pallas kernels  96.5 us (98%)
  local copies, waits for them, and re-layouts  1.32 us (1%)
    pallas_call x1, Pallas kernels, body(): pl.pallas_call(call, out_shape=jax.ShapeDtypeStruct((count, 128), F32), i...  96.5 us

profile of v4, /device:TPU:103, one launch (start us, length us, event | category | flops | bytes accessed | tf_op | source)
XLA Modules:
  0.0 97.8 jit_solution(7292510630133570920)
XLA Ops:
  0.0 96.5 %shard_map.91 = f32[32,128]{1,0:T(8,128)} custom-call(bf16[32,2,64,192]{3,2,1,0:T(8,128)(2,1)} %refs_0_.1, bf16[32,128,128]{2,1,0:T(8,128)(2,1)} %refs_1_.1, bf16[32,64,128]{2,1,0:T(8,128)(2,1)} %refs_2_.1, s32[3,2,32]{2,1,0:T(2,128)} %bitcast.4, s32[2,32]{1,0:T(2,128)} %bitcast.6, s32[1,32]{1,0:T(1,128)} %bitcast.7, f32[32,128]{1,0:T(8,128)} %refs_6_.1, ...), custom_call_target="tpu_custom_call" | custom-call | flops 10000000000 | bytes 4000000 | tf_op jit(solution)/shard_map/pallas_call | solution.py:831
  96.5 1.3 %copy.11 = f32[32,128]{1,0:T(8,128)} copy(f32[32,128]{1,0:T(8,128)} %shard_map.91) | data formatting | bytes 32768

commit v5 on v4

--- a/solution.py
+++ b/solution.py
@@ -129,7 +129,7 @@
     send_in, recv_in, send_small, recv_small, send_obs, recv_obs, smem_sem,
     send_map, recv_map, send_before, recv_before, send_left, recv_left, send_first, recv_first,
     send_mate, recv_mate, send_vec, recv_vec, send_share, recv_share, send_on, recv_on,
-    send_x, recv_x, recv_pair, send_out, recv_out, third_sem, send_end,
+    send_x, recv_x, recv_pair, send_out, recv_out, third_sem, send_end, prior_sem,
 ):
     tm, y = lax.axis_index("tm"), lax.axis_index("state")
     core = lax.rem(tm, 2)
@@ -152,7 +152,10 @@
     end_column = columns_count - 1
     in_master = jnp.where(last_row, column == columns_count - 3, column == master_column(pair))
     at_last_chip = jnp.logical_and(y == 3, jnp.logical_not(single))
-    single_master = jnp.logical_and(y == 3, single)
+    first_column = column == 0
+    merges = column > 0
+    single_master = jnp.logical_and(y == 3, jnp.logical_and(single, merges))
+    exits_first = jnp.logical_and(first_column, y == 3)
     is_master = jnp.logical_and(at_last_chip, in_master)
     is_mate = jnp.logical_and(
         at_last_chip, jnp.logical_and(jnp.logical_not(in_master), column != end_column)
@@ -176,6 +179,13 @@
 
     third_copy = pltpu.make_async_copy(vals_ref.at[:, :, :, pl.ds(128, 64)], third, third_sem)
     third_copy.start()
+    prior_copy = pltpu.make_async_copy(prior_ref, x_in, prior_sem)
+    starts = jnp.logical_and(column == 0, y == 0)
+
+    @pl.when(starts)
+    def _():
+        prior_copy.start()
+
 
     from_single = jnp.logical_and(column > 0, column <= 4)
     from_earlier = jnp.logical_and(second == 0, pair > 2)
@@ -212,7 +222,7 @@
     sends_pair = jnp.logical_or(jnp.logical_and(single_master, column == 3), odd_master)
     peers = (
         7
-        + jnp.where(jnp.logical_or(single_master, is_master), 4, 0)
+        + jnp.where(jnp.logical_or(exits_first, jnp.logical_or(single_master, is_master)), 4, 0)
         + jnp.where(is_mate, 1, 0)
         + jnp.where(odd_master, 4, 0)
         + jnp.where(end_master, 4, 0)
@@ -243,8 +253,8 @@
         start, there = pl.ds(8 * b + CHUNK * q, CHUNK), pl.ds(CHUNK * q, CHUNK)
         return (
             (vals_ref.at[start, :, :, pl.ds(0, 128)], a_buf.at[y, there], 0),
+            (packed.at[start], b_buf.at[y, there], 1),
             (gain_ref.at[start], gain_buf.at[y, there], 2),
-            (packed.at[start], b_buf.at[y, there], 1),
         )
 
     def send_pair(b, src, dst, send, recv):
@@ -279,7 +289,7 @@
 
     def start_chunk(q, carry):
         for b in range(4):
-            for src, dst, kind in big_pairs(b, q)[:2]:
+            for src, dst, kind in big_pairs(b, q)[:1]:
                 send_pair(b, src, dst, send_in.at[b, kind, q], recv_in.at[y, kind, q])
 
         @pl.when(q == 0)
@@ -290,9 +300,10 @@
             for t in range(CHUNK):
                 at = 8 * b + CHUNK * q + t
                 packed[at] = jnp.concatenate([third[at, 0], third[at, 1]], axis=1)
-        for b in range(4):
-            src, dst, kind = big_pairs(b, q)[2]
-            send_pair(b, src, dst, send_in.at[b, kind, q], recv_in.at[y, kind, q])
+        for k in (1, 2):
+            for b in range(4):
+                src, dst, kind = big_pairs(b, q)[k]
+                send_pair(b, src, dst, send_in.at[b, kind, q], recv_in.at[y, kind, q])
         return carry
 
     lax.fori_loop(0, NCHUNK, start_chunk, 0)
@@ -332,7 +343,6 @@
             for j in range(4):
                 arrived(a_buf.at[j, there], recv_in.at[j, 0, q])
                 arrived(b_buf.at[j, there], recv_in.at[j, 1, q])
-                arrived(gain_buf.at[j, there], recv_in.at[j, 2, q])
 
         for j in range(4):
             thirds = b_buf[j, s].astype(F32)
@@ -370,6 +380,13 @@
         image = jnp.concatenate(images, axis=0)
         slot = lax.broadcasted_iota(jnp.int32, (128, NS), 0)
         masked = jnp.where(slot < count, image, 0.0).astype(BF16)
+
+        @pl.when(lax.rem(s, CHUNK) == 0)
+        def _():
+            q = s // CHUNK
+            for j in range(4):
+                arrived(gain_buf.at[j, pl.ds(CHUNK * q, CHUNK)], recv_in.at[j, 2, q])
+
         gains = gain_buf[:, s].reshape(NS, 128)
         correction = jnp.dot(gains, masked, preferred_element_type=F32)
         e_buf[s] = (f_buf[...].reshape(NS, NS) - correction).astype(BF16)
@@ -412,10 +429,6 @@
     q_copy.start()
     arrived(maps_q.at[other], recv_map.at[1])
     arrived(maps.at[other], recv_map.at[0])
-    for h in range(2):
-        total = product(maps.at[1], maps.at[0, core, :, :, pl.ds(128 * h, 128)])
-        chip[4 * core + 2 * h], chip[4 * core + 2 * h + 1] = pack_pair(total)
-
     mine = pl.ds(4 * core, 4)
     theirs = pl.ds(4 * other, 4)
 
@@ -464,15 +477,21 @@
 
         lax.fori_loop(0, 4, one, 0)
 
-    @pl.when(y == 0)
-    def _():
-        chunks(lambda k: chip_before_copy(k).start())
-
-    @pl.when(y == 2)
-    def _():
-        chunks(lambda k: chip_left_copy(k).start())
-
-    @pl.when(lax.rem(y, 2) == 1)
+    for h in range(2):
+        total = product(maps.at[1], maps.at[0, core, :, :, pl.ds(128 * h, 128)])
+        chip[4 * core + 2 * h], chip[4 * core + 2 * h + 1] = pack_pair(total)
+        for k in (2 * h, 2 * h + 1):
+            @pl.when(jnp.logical_and(merges, y == 0))
+            def _():
+                chip_before_copy(k).start()
+
+            @pl.when(jnp.logical_and(merges, y == 2))
+            def _():
+                chip_left_copy(k).start()
+
+    shares_chip = jnp.logical_or(first_column, lax.rem(y, 2) == 1)
+
+    @pl.when(shares_chip)
     def _():
         share(chip, 0).start()
 
@@ -481,19 +500,64 @@
     moved = matvec(block_of_plain(plain_b), rows_of(maps_q.at[0]))
     put_rows(chip_q, sum_rows(moved, rows_of(maps_q.at[1])))
 
-    @pl.when(y == 0)
+    @pl.when(merges & (y == 0))
     def _():
         vec_copies[0].start()
 
-    @pl.when(y == 2)
+    @pl.when(merges & (y == 2))
     def _():
         vec_copies[1].start()
 
-    @pl.when(lax.rem(y, 2) == 1)
+    @pl.when(shares_chip)
     def _():
         shared(chip, 0)
 
-    @pl.when(y == 1)
+    def entry():
+        @pl.when(jnp.logical_or(from_single, jnp.logical_or(from_earlier, from_own)))
+        def _():
+            arrived(x_in, recv_x)
+
+    def apply(plain, vector, shift, out):
+        moved = matvec(block_of_plain(plain), rows_of(vector))
+        put_rows(out, [m + o for m, o in zip(moved, rows_of(shift))])
+
+    def next_pair_copy():
+        there = jnp.where(single, 5, master_column(pair + 1))
+        return remote(x_out, x_pair, send_x.at[8], recv_pair, device(there, 3))
+
+    def next_copy(j):
+        return remote(x_out, x_in, send_x.at[j], recv_x, device(jnp.where(single, column + 1, 2 * pair + 2), j))
+
+    def second_copy(j):
+        return remote(x_mid, x_in, send_x.at[4 + j], recv_x, device(2 * pair + 1, j))
+
+    def end_copy(j):
+        return remote(x_end, x_in, send_end.at[j], recv_x, device(end_column, j))
+
+    along_copy = remote(x_out, x_in, send_end.at[0], recv_x, to_chip(lax.rem(y + 1, 4)))
+
+    @pl.when(first_column)
+    def _():
+        @pl.when(y == 0)
+        def _():
+            prior_copy.wait()
+
+        @pl.when(y > 0)
+        def _():
+            arrived(x_in, recv_x)
+
+        put_rows(x_out, sum_rows(packed_matvec(chip, rows_of(x_in)), rows_of(chip_q)))
+
+        @pl.when(y < 3)
+        def _():
+            along_copy.start()
+
+        @pl.when(y == 3)
+        def _():
+            for j in (3, 2, 1, 0):
+                next_copy(j).start()
+
+    @pl.when(merges & (y == 1))
     def _():
         def one(k):
             n = 4 * core + k
@@ -509,13 +573,13 @@
         vec_copies[2].start()
         vec_copies[3].start()
 
-    @pl.when(y == 2)
+    @pl.when(merges & (y == 2))
     def _():
         arrived(before.at[mine], recv_before.at[4])
         share(before, 1).start()
         arrived(before_q, recv_vec.at[0])
 
-    @pl.when(y == 3)
+    @pl.when(merges & (y == 3))
     def _():
         def one_last(k):
             n = 4 * core + k
@@ -551,32 +615,6 @@
         def _():
             vec_copies[4].start()
 
-    def entry():
-        @pl.when(column == 0)
-        def _():
-            x_in[...] = prior_ref[...]
-
-        @pl.when(jnp.logical_or(from_single, jnp.logical_or(from_earlier, from_own)))
-        def _():
-            arrived(x_in, recv_x)
-
-    def apply(plain, vector, shift, out):
-        moved = matvec(block_of_plain(plain), rows_of(vector))
-        put_rows(out, [m + o for m, o in zip(moved, rows_of(shift))])
-
-    def next_pair_copy():
-        there = jnp.where(single, 5, master_column(pair + 1))
-        return remote(x_out, x_pair, send_x.at[8], recv_pair, device(there, 3))
-
-    def next_copy(j):
-        return remote(x_out, x_in, send_x.at[j], recv_x, device(jnp.where(single, column + 1, 2 * pair + 2), j))
-
-    def second_copy(j):
-        return remote(x_mid, x_in, send_x.at[4 + j], recv_x, device(2 * pair + 1, j))
-
-    def end_copy(j):
-        return remote(x_end, x_in, send_end.at[j], recv_x, device(end_column, j))
-
     @pl.when(single_master)
     def _():
         shared(whole, 4)
@@ -591,7 +629,7 @@
         for j in (3, 2, 1, 0):
             next_copy(j).start()
 
-    @pl.when(y == 3)
+    @pl.when(merges & (y == 3))
     def _():
         shared(left, 3)
 
@@ -620,7 +658,7 @@
         def _():
             one_mate(1)
 
-    @pl.when(y > 0)
+    @pl.when(merges & (y > 0))
     def _():
         shared(before, 1)
         to_plain(before, plain_b)
@@ -677,11 +715,13 @@
     def _():
         arrived(x_in, recv_x)
 
-    @pl.when(y == 0)
+    enters = jnp.logical_or(first_column, y == 0)
+
+    @pl.when(enters)
     def _():
         x_work[...] = x_in[...]
 
-    @pl.when(y > 0)
+    @pl.when(jnp.logical_not(enters))
     def _():
         moved = matvec(block_of_plain(plain_b), rows_of(x_in))
         put_rows(x_work, [m + o for m, o in zip(moved, rows_of(before_q))])
@@ -750,32 +790,43 @@
     map_copy.wait_send()
     q_copy.wait_send()
 
-    @pl.when(y == 0)
+    @pl.when(merges & (y == 0))
     def _():
         chunks(lambda k: chip_before_copy(k).wait_send())
         vec_copies[0].wait_send()
 
-    @pl.when(y == 1)
+    @pl.when(merges & (y == 1))
     def _():
         chunks(lambda k: first_copy(k).wait_send())
         first_before_copy.wait_send()
         vec_copies[2].wait_send()
         vec_copies[3].wait_send()
 
-    @pl.when(y == 2)
+    @pl.when(merges & (y == 2))
     def _():
         chunks(lambda k: chip_left_copy(k).wait_send())
         vec_copies[1].wait_send()
 
-    @pl.when(lax.rem(y, 2) == 1)
+    @pl.when(shares_chip)
     def _():
         share(chip, 0).wait_send()
 
-    @pl.when(y > 0)
+    @pl.when(first_column)
+    def _():
+        @pl.when(y < 3)
+        def _():
+            along_copy.wait_send()
+
+        @pl.when(y == 3)
+        def _():
+            for j in range(4):
+                next_copy(j).wait_send()
+
+    @pl.when(merges & (y > 0))
     def _():
         share(before, 1).wait_send()
 
-    @pl.when(y == 3)
+    @pl.when(merges & (y == 3))
     def _():
         share(last, 2).wait_send()
         share(left, 3).wait_send()
@@ -831,7 +882,7 @@
     return pl.pallas_call(
         call,
         out_shape=jax.ShapeDtypeStruct((count, 128), F32),
-        in_specs=[hbm, hbm, hbm, vmem, vmem, vmem, vmem, vmem, vmem],
+        in_specs=[hbm] * 9,
         out_specs=vmem,
         scratch_shapes=[
             pltpu.VMEM((count, 2, 64, 64), BF16),
@@ -884,7 +935,7 @@
             dma((4,)), dma((4,)), dma((3,)),
             dma((2,)), dma((2,)), dma((5,)), dma((5,)), dma((4,)), dma((4,)), dma((4,)), dma((4,)),
             dma((4,)), dma((2, 4)), dma((5,)), dma((5,)), dma((5,)), dma((5,)), dma((2, 4)), dma((2, 4)),
-            dma((9,)), dma, dma, dma((4,)), dma((4,)), dma, dma((4,)),
+            dma((9,)), dma, dma, dma((4,)), dma((4,)), dma, dma((4,)), dma,
         ],
         compiler_params=pltpu.CompilerParams(
             collective_id=0, has_side_effects=True, vmem_limit_bytes=58 * 1024 * 1024

time: 98.1 us -> 95 us (0.968)
  Pallas kernels: 96.5 us -> 93.4 us
    pallas_call x1, Pallas kernels: 96.5 us -> 93.4 us  [body(): pl.pallas_call(call, out_shape=jax.ShapeDtypeStruct((count, 128), F32), i...]
where the time goes in v5:
time: 95 us; the launch traced here: 94.7 us
  Pallas kernels  93.4 us (98%)
  local copies, waits for them, and re-layouts  1.32 us (1%)
    pallas_call x1, Pallas kernels, body(): pl.pallas_call(call, out_shape=jax.ShapeDtypeStruct((count, 128), F32), i...  93.4 us

profile of v5, /device:TPU:103, one launch (start us, length us, event | category | flops | bytes accessed | tf_op | source)
XLA Modules:
  0.0 94.7 jit_solution(11576115542085896868)
XLA Ops:
  0.0 93.4 %shard_map.91 = f32[32,128]{1,0:T(8,128)} custom-call(bf16[32,2,64,192]{3,2,1,0:T(8,128)(2,1)} %refs_0_.1, bf16[32,128,128]{2,1,0:T(8,128)(2,1)} %refs_1_.1, bf16[32,64,128]{2,1,0:T(8,128)(2,1)} %refs_2_.1, s32[3,2,32]{2,1,0:T(2,128)} %bitcast.4, s32[2,32]{1,0:T(2,128)} %bitcast.6, s32[1,32]{1,0:T(1,128)} %bitcast.7, f32[32,128]{1,0:T(8,128)} %refs_6_.1, ...), custom_call_target="tpu_custom_call" | custom-call | flops 10000000000 | bytes 4000000 | tf_op jit(solution)/shard_map/pallas_call | solution.py:882
  93.4 1.3 %copy.11 = f32[32,128]{1,0:T(8,128)} copy(f32[32,128]{1,0:T(8,128)} %shard_map.91) | data formatting | bytes 32768

commit v6 on v5

--- a/solution.py
+++ b/solution.py
@@ -137,34 +137,28 @@
     first_tm = tm - core
     other = 1 - core
     sibling = (first_tm + other, y)
-    pair, second = column // 2, lax.rem(column, 2)
-    even_pair = lax.rem(pair, 2) == 0
-    last_pair = columns_count // 2 - 1
-
-    def master_column(p):
-        return 2 * p + 1 - lax.rem(p, 2)
+    groups = (columns_count - 4) // 3
+    single = column < 4
+    grouped = jnp.logical_not(single)
+    group = (column - 4) // 3
+    place = column - 4 - 3 * group
+    last_group = group == groups - 1
 
     def device(c, j):
         return 2 * c + core, j
 
-    single = column < 4
-    last_row = column >= columns_count - 4
-    end_column = columns_count - 1
-    in_master = jnp.where(last_row, column == columns_count - 3, column == master_column(pair))
-    at_last_chip = jnp.logical_and(y == 3, jnp.logical_not(single))
     first_column = column == 0
     merges = column > 0
+    at_last_chip = jnp.logical_and(y == 3, grouped)
     single_master = jnp.logical_and(y == 3, jnp.logical_and(single, merges))
     exits_first = jnp.logical_and(first_column, y == 3)
-    is_master = jnp.logical_and(at_last_chip, in_master)
+    is_master = jnp.logical_and(at_last_chip, place == 1)
+    long_master = jnp.logical_and(is_master, jnp.logical_not(last_group))
     is_mate = jnp.logical_and(
-        at_last_chip, jnp.logical_and(jnp.logical_not(in_master), column != end_column)
+        at_last_chip, jnp.logical_or(place == 0, jnp.logical_and(place == 2, jnp.logical_not(last_group)))
     )
-    end_master = jnp.logical_and(is_master, last_row)
-    end_mate = jnp.logical_and(is_mate, column == columns_count - 2)
-    partner = device(jnp.where(last_row, columns_count - 3, column + 1 - 2 * second), 3)
-    mate_column = column + 1 - 2 * second
-    mate_slot = jnp.where(column == columns_count - 2, 1, 0)
+    mate_slot = jnp.where(place == 2, 1, 0)
+    partner = device(5 + 3 * group, 3)
 
     barrier = pltpu.get_barrier_semaphore()
 
@@ -187,46 +181,35 @@
         prior_copy.start()
 
 
-    from_single = jnp.logical_and(column > 0, column <= 4)
-    from_earlier = jnp.logical_and(second == 0, pair > 2)
-    from_own = jnp.logical_and(second == 1, jnp.logical_not(jnp.logical_or(even_pair, single)))
-    earlier_master = device(jnp.where(pair == 2, 3, master_column(pair - 1)), 3)
-
-    @pl.when(from_single)
+    from_before = jnp.logical_or(
+        jnp.logical_and(column > 0, column <= 4), jnp.logical_and(grouped, place == 2)
+    )
+    from_earlier = jnp.logical_and(grouped, jnp.logical_and(place == 0, group > 0))
+    earlier = device(jnp.where(group == 0, 3, 2 + 3 * group), 3)
+
+    @pl.when(from_before)
     def _():
         greet(device(column - 1, 3))
 
-    @pl.when(from_earlier)
-    def _():
-        greet(earlier_master)
-
-    @pl.when(from_own)
-    def _():
-        greet(device(jnp.where(last_row, columns_count - 3, column - 1), 3))
-
-    even_master = jnp.logical_and(is_master, even_pair)
-    odd_master = jnp.logical_and(is_master, jnp.logical_not(even_pair))
-
-    @pl.when(even_master)
-    def _():
-        greet(earlier_master)
+    @pl.when(jnp.logical_or(from_earlier, is_master))
+    def _():
+        greet(earlier)
 
     @pl.when(is_master)
     def _():
-        greet(device(mate_column, 3))
-
-    @pl.when(end_master)
+        greet(device(column - 1, 3))
+
+    @pl.when(long_master)
     def _():
         greet(device(column + 1, 3))
 
-    sends_pair = jnp.logical_or(jnp.logical_and(single_master, column == 3), odd_master)
+    last_single = jnp.logical_and(single_master, column == 3)
     peers = (
         7
         + jnp.where(jnp.logical_or(exits_first, jnp.logical_or(single_master, is_master)), 4, 0)
         + jnp.where(is_mate, 1, 0)
-        + jnp.where(odd_master, 4, 0)
-        + jnp.where(end_master, 4, 0)
-        + jnp.where(sends_pair, 1, 0)
+        + jnp.where(last_single, 1, 0)
+        + jnp.where(long_master, 5, 0)
     )
     pl.semaphore_wait(barrier, peers)
 
@@ -513,7 +496,7 @@
         shared(chip, 0)
 
     def entry():
-        @pl.when(jnp.logical_or(from_single, jnp.logical_or(from_earlier, from_own)))
+        @pl.when(jnp.logical_or(from_before, from_earlier))
         def _():
             arrived(x_in, recv_x)
 
@@ -521,18 +504,17 @@
         moved = matvec(block_of_plain(plain), rows_of(vector))
         put_rows(out, [m + o for m, o in zip(moved, rows_of(shift))])
 
-    def next_pair_copy():
-        there = jnp.where(single, 5, master_column(pair + 1))
-        return remote(x_out, x_pair, send_x.at[8], recv_pair, device(there, 3))
+    def pair_copy(source, there):
+        return remote(source, x_pair, send_x.at[8], recv_pair, device(there, 3))
 
     def next_copy(j):
-        return remote(x_out, x_in, send_x.at[j], recv_x, device(jnp.where(single, column + 1, 2 * pair + 2), j))
-
-    def second_copy(j):
-        return remote(x_mid, x_in, send_x.at[4 + j], recv_x, device(2 * pair + 1, j))
+        return remote(x_out, x_in, send_x.at[j], recv_x, device(column + 1, j))
+
+    def middle_copy(j):
+        return remote(x_mid, x_in, send_x.at[4 + j], recv_x, device(column, j))
 
     def end_copy(j):
-        return remote(x_end, x_in, send_end.at[j], recv_x, device(end_column, j))
+        return remote(x_end, x_in, send_end.at[j], recv_x, device(column + 2, j))
 
     along_copy = remote(x_out, x_in, send_end.at[0], recv_x, to_chip(lax.rem(y + 1, 4)))
 
@@ -622,9 +604,9 @@
         entry()
         apply(plain_a, x_in, whole_q, x_out)
 
-        @pl.when(sends_pair)
-        def _():
-            next_pair_copy().start()
+        @pl.when(last_single)
+        def _():
+            pair_copy(x_out, 5).start()
 
         for j in (3, 2, 1, 0):
             next_copy(j).start()
@@ -654,7 +636,7 @@
 
         one_mate(0)
 
-        @pl.when(last_row)
+        @pl.when(long_master)
         def _():
             one_mate(1)
 
@@ -675,43 +657,32 @@
         def _():
             take_mate(0, plain_d)
 
-            @pl.when(last_row)
+            @pl.when(long_master)
             def _():
                 take_mate(1, plain_e)
 
         entry()
 
-    @pl.when(even_master)
+    @pl.when(is_master)
     def _():
         arrived(x_pair, recv_pair)
         apply(plain_d, x_pair, mate_q.at[0], x_mid)
         apply(plain_a, x_mid, whole_q, x_out)
 
-        @pl.when(last_row)
+        @pl.when(long_master)
         def _():
             apply(plain_e, x_out, mate_q.at[1], x_end)
+            pair_copy(x_end, column + 3).start()
             for j in range(4):
                 end_copy(j).start()
 
-        for j in (3, 2, 1, 0):
+        for j in range(4):
             next_copy(j).start()
         for j in range(3):
-            second_copy(j).start()
+            middle_copy(j).start()
         x_in[...] = x_mid[...]
 
-    @pl.when(odd_master)
-    def _():
-        apply(plain_a, x_in, whole_q, x_mid)
-        apply(plain_d, x_mid, mate_q.at[0], x_out)
-        next_pair_copy().start()
-        for j in range(4):
-            next_copy(j).start()
-        for j in range(4):
-            second_copy(j).start()
-
-    waits_own = jnp.logical_and(jnp.logical_and(even_pair, second == 1), y < 3)
-
-    @pl.when(jnp.logical_and(waits_own, jnp.logical_not(single)))
+    @pl.when(jnp.logical_and(grouped, jnp.logical_and(place == 1, y < 3)))
     def _():
         arrived(x_in, recv_x)
 
@@ -846,21 +817,18 @@
     def _():
         chunks(lambda k: mate_on(k, 0).wait_send())
         for j in range(3):
-            second_copy(j).wait_send()
-
-    @pl.when(end_master)
+            middle_copy(j).wait_send()
+
+    @pl.when(long_master)
     def _():
         chunks(lambda k: mate_on(k, 1).wait_send())
         for j in range(4):
             end_copy(j).wait_send()
-
-    @pl.when(odd_master)
-    def _():
-        second_copy(3).wait_send()
-
-    @pl.when(sends_pair)
-    def _():
-        next_pair_copy().wait_send()
+        pair_copy(x_end, column + 3).wait_send()
+
+    @pl.when(last_single)
+    def _():
+        pair_copy(x_out, 5).wait_send()
 
 
 def body(dyn_cols, dyn_vals, obs_blocks, obs_op, obs_counts, obs_values, gain, sources, prior):

time: 95 us -> 92.1 us (0.969)
  Pallas kernels: 93.4 us -> 90.3 us
    pallas_call x1, Pallas kernels: 93.4 us -> 90.3 us  [body(): pl.pallas_call(call, out_shape=jax.ShapeDtypeStruct((count, 128), F32), i...]
where the time goes in v6:
time: 92.1 us; the launch traced here: 91.7 us
  Pallas kernels  90.3 us (98%)
  local copies, waits for them, and re-layouts  1.32 us (1%)
    pallas_call x1, Pallas kernels, body(): pl.pallas_call(call, out_shape=jax.ShapeDtypeStruct((count, 128), F32), i...  90.3 us

profile of v6, /device:TPU:103, one launch (start us, length us, event | category | flops | bytes accessed | tf_op | source)
XLA Modules:
  0.0 91.7 jit_solution(2601124761160641064)
XLA Ops:
  0.0 90.3 %shard_map.91 = f32[32,128]{1,0:T(8,128)} custom-call(bf16[32,2,64,192]{3,2,1,0:T(8,128)(2,1)} %refs_0_.1, bf16[32,128,128]{2,1,0:T(8,128)(2,1)} %refs_1_.1, bf16[32,64,128]{2,1,0:T(8,128)(2,1)} %refs_2_.1, s32[3,2,32]{2,1,0:T(2,128)} %bitcast.4, s32[2,32]{1,0:T(2,128)} %bitcast.6, s32[1,32]{1,0:T(1,128)} %bitcast.7, f32[32,128]{1,0:T(8,128)} %refs_6_.1, ...), custom_call_target="tpu_custom_call" | custom-call | flops 10000000000 | bytes 4000000 | tf_op jit(solution)/shard_map/pallas_call | solution.py:850
  90.3 1.3 %copy.11 = f32[32,128]{1,0:T(8,128)} copy(f32[32,128]{1,0:T(8,128)} %shard_map.91) | data formatting | bytes 32768

commit v7 on v6

--- a/solution.py
+++ b/solution.py
@@ -11,7 +11,7 @@
 NS = 512
 HALF = 256
 STEPS = 8
-CHUNK = 2
+CHUNK = 1
 NCHUNK = STEPS // CHUNK
 
 
@@ -622,10 +622,33 @@
         share(before, 1).start()
         put_rows(before_q, sum_rows(packed_matvec(left, rows_of(first_q)), rows_of(left_q)))
 
+    def inputs_sent():
+        for b in range(4):
+            @pl.when(jnp.logical_not(is_me(b)))
+            def _():
+                for src, dst, kind in small_pairs(b):
+                    remote(src, dst, send_small.at[b, kind], recv_small.at[y, kind], target_of(b)).wait_send()
+
+        def finish_chunk(q, carry):
+            for b in range(4):
+                @pl.when(jnp.logical_not(is_me(b)))
+                def _():
+                    for src, dst, kind in big_pairs(b, q):
+                        remote(src, dst, send_in.at[b, kind, q], recv_in.at[y, kind, q], target_of(b)).wait_send()
+            return carry
+
+        lax.fori_loop(0, NCHUNK, finish_chunk, 0)
+
+        @pl.when(holds)
+        def _():
+            for mine, others, dst, kind in obs_arrays:
+                remote(others, dst, send_obs.at[kind], recv_obs.at[kind], sibling).wait_send()
+
     @pl.when(is_master)
     def _():
         shared(whole, 4)
         to_plain(whole, plain_a)
+        inputs_sent()
 
         def one_mate(slot):
             def one(k):
@@ -650,6 +673,10 @@
         for k in range(4):
             arrived(mate.at[slot, 4 * other + k], recv_on.at[slot, k])
         to_plain(mate.at[slot], plain)
+
+    @pl.when(jnp.logical_not(is_master))
+    def _():
+        inputs_sent()
 
     @pl.when(jnp.logical_not(single_master))
     def _():
@@ -736,27 +763,6 @@
         @pl.when(jnp.logical_not(own_rows(g)))
         def _():
             remote(sweep_buf.at[g], out_ref.at[here], send_out.at[g], recv_out.at[out_block], (owner, g)).wait_send()
-
-    for b in range(4):
-        @pl.when(jnp.logical_not(is_me(b)))
-        def _():
-            for src, dst, kind in small_pairs(b):
-                remote(src, dst, send_small.at[b, kind], recv_small.at[y, kind], target_of(b)).wait_send()
-
-    def finish_chunk(q, carry):
-        for b in range(4):
-            @pl.when(jnp.logical_not(is_me(b)))
-            def _():
-                for src, dst, kind in big_pairs(b, q):
-                    remote(src, dst, send_in.at[b, kind, q], recv_in.at[y, kind, q], target_of(b)).wait_send()
-        return carry
-
-    lax.fori_loop(0, NCHUNK, finish_chunk, 0)
-
-    @pl.when(holds)
-    def _():
-        for mine, others, dst, kind in obs_arrays:
-            remote(others, dst, send_obs.at[kind], recv_obs.at[kind], sibling).wait_send()
 
     map_copy.wait_send()
     q_copy.wait_send()
@@ -849,7 +855,7 @@
 
     return pl.pallas_call(
         call,
-        out_shape=jax.ShapeDtypeStruct((count, 128), F32),
+        out_shape=pltpu.VMEM((count, 128), F32),
         in_specs=[hbm] * 9,
         out_specs=vmem,
         scratch_shapes=[

time: 92.1 us -> 90.1 us (0.978)
  Pallas kernels: 90.3 us -> 89.1 us
    pallas_call x1, Pallas kernels: 90.3 us -> 89.1 us  [body(): pl.pallas_call(call, out_shape=pltpu.VMEM((count, 128), F32), in_specs=[h...]
where the time goes in v7:
time: 90.1 us; the launch traced here: 89.7 us
  Pallas kernels  89.1 us (99%)
    pallas_call x1, Pallas kernels, body(): pl.pallas_call(call, out_shape=pltpu.VMEM((count, 128), F32), in_specs=[h...  89.1 us

profile of v7, /device:TPU:103, one launch (start us, length us, event | category | flops | bytes accessed | tf_op | source)
XLA Modules:
  0.0 89.7 jit_solution(4001620017001088290)
XLA Ops:
  0.0 89.1 %shard_map.91 = f32[32,128]{1,0:T(8,128)S(1)} custom-call(bf16[32,2,64,192]{3,2,1,0:T(8,128)(2,1)} %refs_0_.1, bf16[32,128,128]{2,1,0:T(8,128)(2,1)} %refs_1_.1, bf16[32,64,128]{2,1,0:T(8,128)(2,1)} %refs_2_.1, s32[3,2,32]{2,1,0:T(2,128)} %bitcast.4, s32[2,32]{1,0:T(2,128)} %bitcast.6, s32[1,32]{1,0:T(1,128)} %bitcast.7, f32[32,128]{1,0:T(8,128)} %refs_6_.1, ...), custom_call_target="tpu_custom_call" | custom-call | flops 10000000000 | bytes 4000000 | tf_op jit(solution)/shard_map/pallas_call | solution.py:856
  89.1 0.6 copy.11

commit v8 on v7

--- a/solution.py
+++ b/solution.py
@@ -91,11 +91,15 @@
     return pack_chunk(parts + pltpu.roll(parts, 64, 1))
 
 
+def plain_pair(packed, n, out):
+    first, second = packed[2 * n].astype(F32), packed[2 * n + 1].astype(F32)
+    first, second = first + pltpu.roll(first, 64, 1), second + pltpu.roll(second, 64, 1)
+    out[:, pl.ds(pl.multiple_of(n * 128, 128), 128)] = jnp.where(left_lanes(first.shape), first, second)
+
+
 def to_plain(packed, out):
     for n in range(4):
-        first, second = packed[2 * n].astype(F32), packed[2 * n + 1].astype(F32)
-        first, second = first + pltpu.roll(first, 64, 1), second + pltpu.roll(second, 64, 1)
-        out[:, n * 128 : (n + 1) * 128] = jnp.where(left_lanes(first.shape), first, second)
+        plain_pair(packed, n, out)
 
 
 def packed_matvec(packed, vector):
@@ -129,7 +133,7 @@
     send_in, recv_in, send_small, recv_small, send_obs, recv_obs, smem_sem,
     send_map, recv_map, send_before, recv_before, send_left, recv_left, send_first, recv_first,
     send_mate, recv_mate, send_vec, recv_vec, send_share, recv_share, send_on, recv_on,
-    send_x, recv_x, recv_pair, send_out, recv_out, third_sem, send_end, prior_sem,
+    send_x, recv_x, recv_pair, send_out, recv_out, third_sem, send_end, prior_sem, send_whole, recv_whole,
 ):
     tm, y = lax.axis_index("tm"), lax.axis_index("state")
     core = lax.rem(tm, 2)
@@ -441,6 +445,20 @@
         n = 4 * core + k
         return remote(whole.at[n], mate.at[mate_slot, n], send_mate.at[k], recv_mate.at[mate_slot, k], partner)
 
+    holds_whole = jnp.logical_or(is_master, single_master)
+
+    def whole_on(k):
+        n = 4 * core + k
+        return remote(whole.at[n], whole.at[n], send_whole.at[k], recv_whole.at[k], sibling)
+
+    def take_whole():
+        for h in range(2):
+            plain_pair(whole, 2 * core + h, plain_a)
+        for k in range(4):
+            arrived(whole.at[4 * other + k], recv_whole.at[k])
+        for h in range(2):
+            plain_pair(whole, 2 * other + h, plain_a)
+
     def mate_on(k, slot):
         n = 4 * core + k
         return remote(mate.at[slot, n], mate.at[slot, n], send_on.at[slot, k], recv_on.at[slot, k], sibling)
@@ -584,11 +602,11 @@
             def _():
                 mate_copy(k).start()
 
+            @pl.when(holds_whole)
+            def _():
+                whole_on(k).start()
+
         chunks(one_whole)
-
-        @pl.when(jnp.logical_or(is_master, single_master))
-        def _():
-            share(whole, 4).start()
 
         arrived(first_q, recv_vec.at[2])
         put_rows(whole_q, sum_rows(packed_matvec(last, rows_of(first_q)), rows_of(whole_q)))
@@ -599,8 +617,7 @@
 
     @pl.when(single_master)
     def _():
-        shared(whole, 4)
-        to_plain(whole, plain_a)
+        take_whole()
         entry()
         apply(plain_a, x_in, whole_q, x_out)
 
@@ -646,22 +663,25 @@
 
     @pl.when(is_master)
     def _():
-        shared(whole, 4)
-        to_plain(whole, plain_a)
+        take_whole()
         inputs_sent()
 
-        def one_mate(slot):
-            def one(k):
-                arrived(mate.at[slot, 4 * core + k], recv_mate.at[slot, k])
-                mate_on(k, slot).start()
-
-            chunks(one)
-
-        one_mate(0)
-
-        @pl.when(long_master)
-        def _():
-            one_mate(1)
+        def one_mate(k, slot, plain):
+            arrived(mate.at[slot, 4 * core + k], recv_mate.at[slot, k])
+            mate_on(k, slot).start()
+
+            @pl.when(lax.rem(k, 2) == 1)
+            def _():
+                plain_pair(mate.at[slot], 2 * core + k // 2, plain)
+
+        def both(k):
+            one_mate(k, 0, plain_d)
+
+            @pl.when(long_master)
+            def _():
+                one_mate(k, 1, plain_e)
+
+        chunks(both)
 
     @pl.when(merges & (y > 0))
     def _():
@@ -672,7 +692,8 @@
         arrived(mate_q.at[slot], recv_vec.at[3 + slot])
         for k in range(4):
             arrived(mate.at[slot, 4 * other + k], recv_on.at[slot, k])
-        to_plain(mate.at[slot], plain)
+        for h in range(2):
+            plain_pair(mate.at[slot], 2 * other + h, plain)
 
     @pl.when(jnp.logical_not(is_master))
     def _():
@@ -815,7 +836,7 @@
 
     @pl.when(jnp.logical_or(is_master, single_master))
     def _():
-        share(whole, 4).wait_send()
+        chunks(lambda k: whole_on(k).wait_send())
         for j in range(4):
             next_copy(j).wait_send()
 
@@ -909,7 +930,7 @@
             dma((4,)), dma((4,)), dma((3,)),
             dma((2,)), dma((2,)), dma((5,)), dma((5,)), dma((4,)), dma((4,)), dma((4,)), dma((4,)),
             dma((4,)), dma((2, 4)), dma((5,)), dma((5,)), dma((5,)), dma((5,)), dma((2, 4)), dma((2, 4)),
-            dma((9,)), dma, dma, dma((4,)), dma((4,)), dma, dma((4,)), dma,
+            dma((9,)), dma, dma, dma((4,)), dma((4,)), dma, dma((4,)), dma, dma((4,)), dma((4,)),
         ],
         compiler_params=pltpu.CompilerParams(
             collective_id=0, has_side_effects=True, vmem_limit_bytes=58 * 1024 * 1024

time: 90.1 us -> 89.9 us (level)
  no operation moved by 1% of the time
where the time goes in v8:
time: 89.9 us; the launch traced here: 89.6 us
  Pallas kernels  89 us (99%)
    pallas_call x1, Pallas kernels, body(): pl.pallas_call(call, out_shape=pltpu.VMEM((count, 128), F32), in_specs=[h...  89 us

profile of v8, /device:TPU:103, one launch (start us, length us, event | category | flops | bytes accessed | tf_op | source)
XLA Modules:
  0.0 89.6 jit_solution(16690477111245359827)
XLA Ops:
  0.0 89.0 %shard_map.91 = f32[32,128]{1,0:T(8,128)S(1)} custom-call(bf16[32,2,64,192]{3,2,1,0:T(8,128)(2,1)} %refs_0_.1, bf16[32,128,128]{2,1,0:T(8,128)(2,1)} %refs_1_.1, bf16[32,64,128]{2,1,0:T(8,128)(2,1)} %refs_2_.1, s32[3,2,32]{2,1,0:T(2,128)} %bitcast.4, s32[2,32]{1,0:T(2,128)} %bitcast.6, s32[1,32]{1,0:T(1,128)} %bitcast.7, f32[32,128]{1,0:T(8,128)} %refs_6_.1, ...), custom_call_target="tpu_custom_call" | custom-call | flops 10000000000 | bytes 4000000 | tf_op jit(solution)/shard_map/pallas_call | solution.py:877
  89.0 0.6 copy.11

commit v9 on v8

--- a/solution.py
+++ b/solution.py
@@ -53,13 +53,12 @@
     return load
 
 
-def product(left, right):
+def half_product(left, right, h):
+    rows = pl.ds(h * HALF, HALF)
     total = None
-    for h in range(2):
-        rows = pl.ds(h * HALF, HALF)
-        for a, b in ((0, 0), (0, 1), (1, 0)):
-            term = jnp.dot(left[h, a], right[b, rows, :], preferred_element_type=F32)
-            total = term if total is None else total + term
+    for a, b in ((0, 0), (0, 1), (1, 0)):
+        term = jnp.dot(left[h, a], right[b, rows, :], preferred_element_type=F32)
+        total = term if total is None else total + term
     return total
 
 
@@ -410,12 +409,14 @@
 
     lax.fori_loop(0, STEPS, step, 0)
 
-    map_copy = remote(maps.at[core], maps.at[core], send_map.at[0], recv_map.at[0], sibling)
+    def map_copy(h, k):
+        return remote(maps.at[core, h], maps.at[core, h], send_map.at[k], recv_map.at[k], sibling)
+
     q_copy = remote(maps_q.at[core], maps_q.at[core], send_map.at[1], recv_map.at[1], sibling)
-    map_copy.start()
+    map_copy(other, 0).start()
+    map_copy(core, 2).start()
     q_copy.start()
-    arrived(maps_q.at[other], recv_map.at[1])
-    arrived(maps.at[other], recv_map.at[0])
+    arrived(maps.at[other, core], recv_map.at[0])
     mine = pl.ds(4 * core, 4)
     theirs = pl.ds(4 * other, 4)
 
@@ -478,8 +479,18 @@
 
         lax.fori_loop(0, 4, one, 0)
 
+    def right(h):
+        return maps.at[0, core, :, :, pl.ds(128 * h, 128)]
+
     for h in range(2):
-        total = product(maps.at[1], maps.at[0, core, :, :, pl.ds(128 * h, 128)])
+        plain_c[:, h * 128 : (h + 1) * 128] = half_product(maps.at[1], right(h), 0)
+
+    @pl.when(core == 0)
+    def _():
+        arrived(maps.at[other, other], recv_map.at[2])
+
+    for h in range(2):
+        total = plain_c[:, h * 128 : (h + 1) * 128] + half_product(maps.at[1], right(h), 1)
         chip[4 * core + 2 * h], chip[4 * core + 2 * h + 1] = pack_pair(total)
         for k in (2 * h, 2 * h + 1):
             @pl.when(jnp.logical_and(merges, y == 0))
@@ -496,6 +507,11 @@
     def _():
         share(chip, 0).start()
 
+    @pl.when(core == 1)
+    def _():
+        arrived(maps.at[other, other], recv_map.at[2])
+
+    arrived(maps_q.at[other], recv_map.at[1])
     half_map(maps.at[0], plain_c)
     half_map(maps.at[1], plain_b)
     moved = matvec(block_of_plain(plain_b), rows_of(maps_q.at[0]))
@@ -785,7 +801,8 @@
         def _():
             remote(sweep_buf.at[g], out_ref.at[here], send_out.at[g], recv_out.at[out_block], (owner, g)).wait_send()
 
-    map_copy.wait_send()
+    map_copy(other, 0).wait_send()
+    map_copy(core, 2).wait_send()
     q_copy.wait_send()
 
     @pl.when(merges & (y == 0))
@@ -928,7 +945,7 @@
             dma((4, 3, NCHUNK)), dma((4, 3, NCHUNK)),
             dma((4, 2)), dma((4, 2)),
             dma((4,)), dma((4,)), dma((3,)),
-            dma((2,)), dma((2,)), dma((5,)), dma((5,)), dma((4,)), dma((4,)), dma((4,)), dma((4,)),
+            dma((3,)), dma((3,)), dma((5,)), dma((5,)), dma((4,)), dma((4,)), dma((4,)), dma((4,)),
             dma((4,)), dma((2, 4)), dma((5,)), dma((5,)), dma((5,)), dma((5,)), dma((2, 4)), dma((2, 4)),
             dma((9,)), dma, dma, dma((4,)), dma((4,)), dma, dma((4,)), dma, dma((4,)), dma((4,)),
         ],

time: 89.9 us -> 89.3 us (level)
  no operation moved by 1% of the time
where the time goes in v9:
time: 89.3 us; the launch traced here: 89 us
  Pallas kernels  88.3 us (99%)
    pallas_call x1, Pallas kernels, body(): pl.pallas_call(call, out_shape=pltpu.VMEM((count, 128), F32), in_specs=[h...  88.3 us

profile of v9, /device:TPU:103, one launch (start us, length us, event | category | flops | bytes accessed | tf_op | source)
XLA Modules:
  0.0 89.0 jit_solution(893316223734240673)
XLA Ops:
  0.0 88.3 %shard_map.91 = f32[32,128]{1,0:T(8,128)S(1)} custom-call(bf16[32,2,64,192]{3,2,1,0:T(8,128)(2,1)} %refs_0_.1, bf16[32,128,128]{2,1,0:T(8,128)(2,1)} %refs_1_.1, bf16[32,64,128]{2,1,0:T(8,128)(2,1)} %refs_2_.1, s32[3,2,32]{2,1,0:T(2,128)} %bitcast.4, s32[2,32]{1,0:T(2,128)} %bitcast.6, s32[1,32]{1,0:T(1,128)} %bitcast.7, f32[32,128]{1,0:T(8,128)} %refs_6_.1, ...), custom_call_target="tpu_custom_call" | custom-call | flops 10000000000 | bytes 4000000 | tf_op jit(solution)/shard_map/pallas_call | solution.py:894
  88.3 0.6 copy.11

commit v10 on v9

--- a/solution.py
+++ b/solution.py
@@ -319,6 +319,9 @@
 
     maps_q[core] = jnp.zeros((4, 128), F32)
 
+    def map_copy(h, k):
+        return remote(maps.at[core, h], maps.at[core, h], send_map.at[k], recv_map.at[k], sibling)
+
     def step(s, carry):
         at = first_step + s
 
@@ -399,22 +402,21 @@
 
         @pl.when(s > 0)
         def _():
-            for h in range(2):
+            for h, k in ((other, 0), (core, 2)):
                 matrix = e_buf[s]
                 value = jnp.dot(matrix, maps[core, h, 0], preferred_element_type=F32)
                 value = value + jnp.dot(matrix, maps[core, h, 1], preferred_element_type=F32)
                 maps[core, h, 0], maps[core, h, 1] = split(value)
 
+                @pl.when(s == STEPS - 1)
+                def _():
+                    map_copy(h, k).start()
+
         return carry
 
     lax.fori_loop(0, STEPS, step, 0)
 
-    def map_copy(h, k):
-        return remote(maps.at[core, h], maps.at[core, h], send_map.at[k], recv_map.at[k], sibling)
-
     q_copy = remote(maps_q.at[core], maps_q.at[core], send_map.at[1], recv_map.at[1], sibling)
-    map_copy(other, 0).start()
-    map_copy(core, 2).start()
     q_copy.start()
     arrived(maps.at[other, core], recv_map.at[0])
     mine = pl.ds(4 * core, 4)

time: 89.3 us -> 89.3 us (level)
  no operation moved by 1% of the time
where the time goes in v10:
time: 89.3 us; the launch traced here: 88.9 us
  Pallas kernels  88.3 us (99%)
    pallas_call x1, Pallas kernels, body(): pl.pallas_call(call, out_shape=pltpu.VMEM((count, 128), F32), in_specs=[h...  88.3 us

profile of v10, /device:TPU:103, one launch (start us, length us, event | category | flops | bytes accessed | tf_op | source)
XLA Modules:
  0.0 88.9 jit_solution(10111414599461225879)
XLA Ops:
  0.0 88.3 %shard_map.91 = f32[32,128]{1,0:T(8,128)S(1)} custom-call(bf16[32,2,64,192]{3,2,1,0:T(8,128)(2,1)} %refs_0_.1, bf16[32,128,128]{2,1,0:T(8,128)(2,1)} %refs_1_.1, bf16[32,64,128]{2,1,0:T(8,128)(2,1)} %refs_2_.1, s32[3,2,32]{2,1,0:T(2,128)} %bitcast.4, s32[2,32]{1,0:T(2,128)} %bitcast.6, s32[1,32]{1,0:T(1,128)} %bitcast.7, f32[32,128]{1,0:T(8,128)} %refs_6_.1, ...), custom_call_target="tpu_custom_call" | custom-call | flops 10000000000 | bytes 4000000 | tf_op jit(solution)/shard_map/pallas_call | solution.py:896
  88.3 0.6 copy.11
